TPU v7x, 32 devices: a whole 2x2x4 slice. The times are simulated.
32 devices in a mesh: shift: 4 (over x, core), space: 8 (over z, y).
Axes of the slice: x: 2, y: 2, z: 4, core: 2. Of those that a mesh axis runs over, the one named last changes fastest.
Arguments:
- labels: int32 [16, 32, 256], P('space'), may hold values from 0 to 7
- conductance: float32 [8], replicated, may hold values from 0.2 to 5
- capacity_table: float32 [8], replicated, may hold values from 0.5 to 2
- shift_values: float32 [8], replicated, may hold values from 0.1 to 4
- prior_basis: float32 [256, 16, 32, 256], P(None, 'space', 'shift'), may hold values from -6 to 6
Outputs:
- new_block: float32 [8, 8, 16, 32, 256], P(None, None, 'space', 'shift')
- coefficients: float32 [64, 256], replicated
- factor: float32 [64, 64], replicated
All inputs are finite; a program needn't handle non-finite values.
Results may differ from a plain program's by a relative error of at most 0.0003.
Values sent between devices are 32-bit elements; how exact they have to be, the bound alone decides.
A program may use at most 64 MiB of HBM per device.

v0:
```python
import jax
import jax.numpy as jnp
from jax import lax
from jax.sharding import PartitionSpec as P

COLS = 8
SWEEPS = 4


LOWER_BOUND = 0.1
UPPER_BOUND = 2.0


def padded_2(cells, sides, width):
    for axis, dim in sides:
        count = lax.axis_size(axis)
        ends = count - 1
        head = lax.slice_in_dim(cells, 0, width, axis=dim)
        tail = lax.slice_in_dim(cells, cells.shape[dim] - width, cells.shape[dim], axis=dim)
        cells = jnp.concatenate(
            [
                lax.ppermute(tail, axis, [(i, (i + 1) % count) for i in range(ends)]),
                cells,
                lax.ppermute(head, axis, [((i + 1) % count, i) for i in range(ends)]),
            ],
            axis=dim,
        )
    return cells


def lookup(labels, table):
    materials = jnp.arange(table.shape[0], dtype=jnp.int32)
    onehot = (labels[None] == materials[:, None, None, None]).astype(jnp.float32)
    return jnp.sum(onehot * table[:, None, None, None], axis=0)


def conductances(conduct, padded):
    west_face = 0.5 * (conduct + padded[:-2, 1:-1, 1:-1])
    east_face = 0.5 * (conduct + padded[2:, 1:-1, 1:-1])
    south_face = 0.5 * (conduct + padded[1:-1, :-2, 1:-1])
    north_face = 0.5 * (conduct + padded[1:-1, 2:, 1:-1])
    below_face = 0.5 * (conduct + padded[1:-1, 1:-1, :-2])
    above_face = 0.5 * (conduct + padded[1:-1, 1:-1, 2:])
    return (west_face, east_face, south_face, north_face, below_face, above_face)


def neighbours(padded, face_list):
    west_face, east_face, south_face, north_face, below_face, above_face = face_list
    summed = west_face * padded[..., :-2, 1:-1, 1:-1] + east_face * padded[..., 2:, 1:-1, 1:-1]
    summed = (
        summed
        + south_face * padded[..., 1:-1, :-2, 1:-1]
        + north_face * padded[..., 1:-1, 2:, 1:-1]
    )
    summed = (
        summed
        + below_face * padded[..., 1:-1, 1:-1, :-2]
        + above_face * padded[..., 1:-1, 1:-1, 2:]
    )
    return summed


def diagonal_of(face_list, shift_list, capacity):
    west_face, east_face, south_face, north_face, below_face, above_face = face_list
    summed = west_face + east_face + (south_face + north_face) + (below_face + above_face)
    return summed[None, None] + shift_list[:, None, None, None, None] * capacity[None, None]


def chebyshev(source, face_list, diagonal, padder):
    center = 0.5 * (UPPER_BOUND + LOWER_BOUND)
    spread = 0.5 * (UPPER_BOUND - LOWER_BOUND)
    ratio_value = center / spread
    reciprocal = 1.0 / diagonal
    solution = jnp.zeros_like(source)
    remainder = source
    weight_old = 1.0 / ratio_value
    direction = reciprocal * remainder / center
    for sweep_index in range(SWEEPS):
        solution = solution + direction
        if sweep_index + 1 < SWEEPS:
            applied = diagonal * direction - neighbours(padder(direction), face_list)
            remainder = remainder - applied
            weight_new = 1.0 / (2.0 * ratio_value - weight_old)
            direction = weight_new * weight_old * direction + 2.0 * weight_new / spread * (
                reciprocal * remainder
            )
            weight_old = weight_new
    return solution


def products(left_side, right_side):
    return lax.dot_general(
        left_side, right_side, (((1,), (1,)), ((), ())), precision=lax.Precision.HIGHEST
    )


def matmul(left_side, right_side):
    return jnp.dot(left_side, right_side, precision=lax.Precision.HIGHEST)


def local(labels, conductance, capacity_table, shift_values, prior_basis):
    groups = lax.axis_size("shift")
    shifts_all = shift_values.shape[0]
    per_device = shifts_all // groups
    new_count = shifts_all * COLS
    basis_count = prior_basis.shape[0]
    slab_x = prior_basis.shape[1]
    quarter = prior_basis.shape[2]
    depth = prior_basis.shape[3]
    flat_basis = prior_basis.reshape(basis_count, slab_x * quarter * depth)
    cell_weight = 1.0 / (slab_x * quarter * depth * groups * lax.axis_size("space"))
    tail_columns = prior_basis[basis_count - new_count :]
    conduct = lookup(labels, conductance)
    capacity = lookup(labels, capacity_table)
    rimmed = padded_2(conduct, (("space", 0),), 1)
    face_list = conductances(conduct, jnp.pad(rimmed, ((0, 0), (1, 1), (1, 1))))
    shift_list = lax.dynamic_slice_in_dim(
        shift_values, lax.axis_index("shift") * per_device, per_device, 0
    )
    diagonal = diagonal_of(face_list, shift_list, capacity)
    starting = lax.all_to_all(tail_columns, "shift", split_axis=0, concat_axis=2, tiled=True)
    full_y = starting.shape[2]
    source = starting.reshape(per_device, COLS, slab_x, full_y, depth) * capacity[None, None]

    def padder(field):
        widened = padded_2(field, (("space", 2),), 1)
        return jnp.pad(widened, ((0, 0), (0, 0), (0, 0), (1, 1), (1, 1)))

    fields = chebyshev(source, face_list, diagonal, padder)
    merged = fields.reshape(per_device * COLS, slab_x, full_y, depth)
    regrouped = lax.all_to_all(merged, "shift", split_axis=2, concat_axis=0, tiled=True)
    columns = regrouped.reshape(new_count, slab_x * quarter * depth)
    first_proj = lax.psum(products(columns, flat_basis), ("shift", "space")) * cell_weight
    columns = columns - matmul(first_proj, flat_basis)
    second_proj = lax.psum(products(columns, flat_basis), ("shift", "space")) * cell_weight
    columns = columns - matmul(second_proj, flat_basis)
    gram_matrix = lax.psum(products(columns, columns), ("shift", "space")) * cell_weight
    factor = jnp.linalg.cholesky(gram_matrix)
    orthonormal = lax.linalg.triangular_solve(factor, columns, left_side=True, lower=True)
    new_block = orthonormal.reshape(shifts_all, COLS, slab_x, quarter, depth)
    return (new_block, first_proj + second_proj, factor)


def solution(mesh):
    in_specs = (P("space", None, None), P(), P(), P(), P(None, "space", "shift", None))
    out_specs = (P(None, None, "space", "shift", None), P(), P())
    return jax.shard_map(local, mesh=mesh, in_specs=in_specs, out_specs=out_specs, check_vma=False)
```

profile of v0, /device:TPU:0, one launch (start us, length us, event | category | flops | bytes accessed | tf_op | source)
XLA Modules:
  0.0 465.4 jit_solution(4275959018128577035)
XLA Ops:
  7.2 2.3 slice.133
  9.5 4.2 all-to-all-start
  13.9 4.2 collective-permute-start
  19.7 4.2 collective-permute-done.1
  24.3 3.9 all-to-all-done
  28.6 4.2 collective-permute-start.2
  34.1 20.9 %collective-permute-done.2 = f32[2,8,1,32,256]{4,3,2,1,0:T(8,128)S(1)} collective-permute-done((f32[2,8,1,32,256]{4,3,2,1,0:T(8,128)S(1)}, f32[2,8,1,32,256]{4,3,2,1,0:T(8,128)S(1)}, u32[]{:S(2)}, u32[]{:S(2)}) %collective-permute-start.2) | collective-permute-done | bytes 524320 | tf_op jit(solution)/shard_map/ppermute | solution.py:22
  54.9 1.8 select_maximum_fusion.4
  58.1 4.4 collective-permute-start.4
  63.8 20.0 %collective-permute-done.4 = f32[2,8,1,32,256]{4,3,2,1,0:T(8,128)S(1)} collective-permute-done((f32[2,8,1,32,256]{4,3,2,1,0:T(8,128)S(1)}, f32[2,8,1,32,256]{4,3,2,1,0:T(8,128)S(1)}, u32[]{:S(2)}, u32[]{:S(2)}) %collective-permute-start.4) | collective-permute-done | bytes 524320 | tf_op jit(solution)/shard_map/ppermute | solution.py:22
  86.9 4.4 collective-permute-start.6
  92.6 19.0 %collective-permute-done.6 = f32[2,8,1,32,256]{4,3,2,1,0:T(8,128)S(1)} collective-permute-done((f32[2,8,1,32,256]{4,3,2,1,0:T(8,128)S(1)}, f32[2,8,1,32,256]{4,3,2,1,0:T(8,128)S(1)}, u32[]{:S(2)}, u32[]{:S(2)}) %collective-permute-start.6) | collective-permute-done | bytes 524320 | tf_op jit(solution)/shard_map/ppermute | solution.py:22
  116.6 3.5 all-to-all-start.1
  120.4 7.9 %copy.46 = f32[32,8,16,256]{3,1,2,0:T(8,128)} copy(f32[32,8,16,256]{3,2,1,0:T(8,128)} %bitcast.53) | data formatting | bytes 8388608
  128.3 6.3 %all-to-all-done.1 = f32[16,2,32,256]{3,1,0,2:T(2,128)S(1)} async-done(((f32[16,2,32,256]{3,1,0,2:T(2,128)}), f32[16,2,32,256]{3,1,0,2:T(2,128)S(1)}, u32[]{:S(2)}, u32[]{:S(2)}) %all-to-all-start.1) | async-done | bytes 1048608 | tf_op jit(solution)/shard_map/all_to_all | solution.py:131
  135.5 6.8 %fusion.71 = f32[64,256]{1,0:T(8,128)} fusion(f32[64,4096]{1,0:T(8,128)S(1)} %reshape.60, f32[256,4096]{1,0:T(8,128)} %bitcast.45), kind=kOutput, calls=%fused_computation.123 | convolution fusion | flops 805306368 | bytes 5308416 | tf_op jit(solution)/shard_map/dot_general | solution.py:92
  142.6 123.9 %all-reduce.7.cloned.1.call-done = f32[64,256]{1,0:T(8,128)} async-done(((f32[64,256]{1,0:T(8,128)}), f32[64,256]{1,0:T(8,128)}) %all-reduce.7.cloned.1.call-update) | async-done | bytes 65552 | tf_op jit(solution)/shard_map/psum | solution.py:133
  266.5 5.0 %convolution_subtract_fusion.1 = f32[64,4096]{1,0:T(8,128)S(1)} fusion(f32[64,4096]{1,0:T(8,128)S(1)} %reshape.60, f32[256,4096]{1,0:T(8,128)} %bitcast.46, f32[64,256]{1,0:T(8,128)} %all-reduce.7.cloned.1.call-done), kind=kOutput, calls=%fused_computation.5 | convolution fusion | flops 805584896 | bytes 6356992 | tf_op jit(solution)/shard_map/dot_general | solution.py:98
  271.5 4.6 fusion.72
  276.1 118.5 %all-reduce.9.cloned.1.call-done = f32[64,256]{1,0:T(8,128)} async-done(((f32[64,256]{1,0:T(8,128)}), f32[64,256]{1,0:T(8,128)}) %all-reduce.9.cloned.1.call-update) | async-done | bytes 65552 | tf_op jit(solution)/shard_map/psum | solution.py:135
  394.7 4.8 %convolution_subtract_fusion = f32[64,4096]{1,0:T(8,128)S(1)} fusion(f32[64,4096]{1,0:T(8,128)S(1)} %convolution_subtract_fusion.1, f32[256,4096]{1,0:T(8,128)} %bitcast.47, f32[64,256]{1,0:T(8,128)} %all-reduce.9.cloned.1.call-done), kind=kOutput, calls=%fused_computation.4 | convolution fusion | flops 805584896 | bytes 6356992 | tf_op jit(solution)/shard_map/dot_general | solution.py:98
  400.5 41.3 %psum.23 = f32[64,64]{0,1:T(8,128)S(1)} all-reduce(f32[64,64]{0,1:T(8,128)S(1)} %fusion.73), channel_id=1, replica_groups=mesh['shift'=4,'space'=8] {'shift','space'}, use_global_device_ids=true, to_apply=%region_4.5 | all-reduce | flops 4096 | bytes 32768 | tf_op jit(solution)/shard_map/psum | solution.py:137
  441.9 5.8 %cholesky.16 = f32[64,64]{1,0:T(8,128)S(1)} custom-call(f32[64,64]{1,0:T(8,128)S(1)} %fusion.54), custom_call_target="Cholesky" | custom-call | tf_op jit(solution)/shard_map/jit(cholesky)/cholesky | solution.py:138
  449.7 4.9 %custom-call.6 = f32[1,64,64]{1,2,0:T(8,128)S(1)} custom-call(f32[1,64,64]{2,1,0:T(8,128)S(1)} %get-tuple-element.20), custom_call_target="InvertDiagBlocksLowerTriangular" | custom-call | tf_op jit(solution)/shard_map/triangular_solve | solution.py:139
  (58 shorter events, 24.1 us)
Async XLA Ops:
  7.2 6.6 %copy-start.5 = (f32[8]{0:T(128)S(1)}, f32[8]{0:T(128)}, u32[]{:S(2)}) copy-start(f32[8]{0:T(128)} %param.7) | copy-start | bytes 100
  7.2 6.5 %copy-start.4 = (f32[8]{0:T(128)S(1)}, f32[8]{0:T(128)}, u32[]{:S(2)}) copy-start(f32[8]{0:T(128)} %param.6) | copy-start | bytes 100
  7.2 6.5 %copy-start.3 = (s32[2,32,256]{2,1,0:T(8,128)S(1)}, s32[2,32,256]{2,1,0:T(8,128)}, u32[]{:S(2)}) copy-start(s32[2,32,256]{2,1,0:T(8,128)} %param.5) | copy-start | bytes 196612
  7.2 12.2 %copy-start.6 = (f32[8]{0:T(128)S(1)}, f32[8]{0:T(128)}, u32[]{:S(2)}) copy-start(f32[8]{0:T(128)} %param.8) | copy-start | bytes 100
  9.5 18.7 %all-to-all-start = ((f32[64,2,8,256]{3,2,1,0:T(8,128)}), f32[64,2,8,256]{3,2,1,0:T(8,128)S(1)}, u32[]{:S(2)}, u32[]{:S(2)}) async-start(f32[64,2,8,256]{3,2,1,0:T(8,128)} %slice.133), calls=%async_computation | async-start | bytes 2097152 | tf_op jit(solution)/shard_map/all_to_all | solution.py:121
  13.9 5.8 %collective-permute-start = (f32[1,32,256]{2,1,0:T(8,128)S(1)}, f32[1,32,256]{2,1,0:T(8,128)S(1)}, u32[]{:S(2)}, u32[]{:S(2)}) collective-permute-start(f32[1,32,256]{2,1,0:T(8,128)S(1)} %get-tuple-element.42), channel_id=1, source_target_pairs={{0,1},{1,2},{2,3},{3,4},{4,5},{5,6},{6,7},{8,9},{9,10},{10,11},{11... | collective-permute-start | bytes 98312 | tf_op jit(solution)/shard_map/ppermute | solution.py:22
  18.1 5.8 %collective-permute-start.1 = (f32[1,32,256]{2,1,0:T(8,128)S(1)}, f32[1,32,256]{2,1,0:T(8,128)S(1)}, u32[]{:S(2)}, u32[]{:S(2)}) collective-permute-start(f32[1,32,256]{2,1,0:T(8,128)S(1)} %get-tuple-element.43), channel_id=1, source_target_pairs={{1,0},{2,1},{3,2},{4,3},{5,4},{6,5},{7,6},{9,8},{10,9},{11,10},{12... | collective-permute-start | bytes 98312 | tf_op jit(solution)/shard_map/ppermute | solution.py:24
  28.6 26.4 %collective-permute-start.2 = (f32[2,8,1,32,256]{4,3,2,1,0:T(8,128)S(1)}, f32[2,8,1,32,256]{4,3,2,1,0:T(8,128)S(1)}, u32[]{:S(2)}, u32[]{:S(2)}) collective-permute-start(f32[2,8,1,32,256]{4,3,2,1,0:T(8,128)S(1)} %get-tuple-element.37), channel_id=1, source_target_pairs={{0,1},{1,2},{2,3},{3,4},{4,5},{5,6},{6,7},{8,9},{9,10},{10,11},{11... | collective-permute-start | bytes 1572872 | tf_op jit(solution)/shard_map/ppermute | solution.py:22
  32.8 22.2 %collective-permute-start.3 = (f32[2,8,1,32,256]{4,3,2,1,0:T(8,128)S(1)}, f32[2,8,1,32,256]{4,3,2,1,0:T(8,128)S(1)}, u32[]{:S(2)}, u32[]{:S(2)}) collective-permute-start(f32[2,8,1,32,256]{4,3,2,1,0:T(8,128)S(1)} %get-tuple-element.38), channel_id=1, source_target_pairs={{1,0},{2,1},{3,2},{4,3},{5,4},{6,5},{7,6},{9,8},{10,9},{11,10},{12... | collective-permute-start | bytes 1572872 | tf_op jit(solution)/shard_map/ppermute | solution.py:24
  58.1 25.7 %collective-permute-start.4 = (f32[2,8,1,32,256]{4,3,2,1,0:T(8,128)S(1)}, f32[2,8,1,32,256]{4,3,2,1,0:T(8,128)S(1)}, u32[]{:S(2)}, u32[]{:S(2)}) collective-permute-start(f32[2,8,1,32,256]{4,3,2,1,0:T(8,128)S(1)} %get-tuple-element.35), channel_id=1, source_target_pairs={{0,1},{1,2},{2,3},{3,4},{4,5},{5,6},{6,7},{8,9},{9,10},{10,11},{11... | collective-permute-start | bytes 1572872 | tf_op jit(solution)/shard_map/ppermute | solution.py:22
  62.5 21.3 %collective-permute-start.5 = (f32[2,8,1,32,256]{4,3,2,1,0:T(8,128)S(1)}, f32[2,8,1,32,256]{4,3,2,1,0:T(8,128)S(1)}, u32[]{:S(2)}, u32[]{:S(2)}) collective-permute-start(f32[2,8,1,32,256]{4,3,2,1,0:T(8,128)S(1)} %get-tuple-element.36), channel_id=1, source_target_pairs={{1,0},{2,1},{3,2},{4,3},{5,4},{6,5},{7,6},{9,8},{10,9},{11,10},{12... | collective-permute-start | bytes 1572872 | tf_op jit(solution)/shard_map/ppermute | solution.py:24
  86.9 24.8 %collective-permute-start.6 = (f32[2,8,1,32,256]{4,3,2,1,0:T(8,128)S(1)}, f32[2,8,1,32,256]{4,3,2,1,0:T(8,128)S(1)}, u32[]{:S(2)}, u32[]{:S(2)}) collective-permute-start(f32[2,8,1,32,256]{4,3,2,1,0:T(8,128)S(1)} %get-tuple-element.33), channel_id=1, source_target_pairs={{0,1},{1,2},{2,3},{3,4},{4,5},{5,6},{6,7},{8,9},{9,10},{10,11},{11... | collective-permute-start | bytes 1572872 | tf_op jit(solution)/shard_map/ppermute | solution.py:22
  91.3 20.4 %collective-permute-start.7 = (f32[2,8,1,32,256]{4,3,2,1,0:T(8,128)S(1)}, f32[2,8,1,32,256]{4,3,2,1,0:T(8,128)S(1)}, u32[]{:S(2)}, u32[]{:S(2)}) collective-permute-start(f32[2,8,1,32,256]{4,3,2,1,0:T(8,128)S(1)} %get-tuple-element.34), channel_id=1, source_target_pairs={{1,0},{2,1},{3,2},{4,3},{5,4},{6,5},{7,6},{9,8},{10,9},{11,10},{12... | collective-permute-start | bytes 1572872 | tf_op jit(solution)/shard_map/ppermute | solution.py:24
  116.6 18.0 %all-to-all-start.1 = ((f32[16,2,32,256]{3,1,0,2:T(2,128)}), f32[16,2,32,256]{3,1,0,2:T(2,128)S(1)}, u32[]{:S(2)}, u32[]{:S(2)}) async-start(f32[16,2,32,256]{3,1,0,2:T(2,128)} %copy.36), calls=%async_computation.1 | async-start | bytes 2097152 | tf_op jit(solution)/shard_map/all_to_all | solution.py:131
  120.1 146.4 %all-reduce.7.cloned.1.call-start = ((), (), s32[]{:S(2)}) async-start(), calls=%async_computation.2 | async-start | bytes 131072 | tf_op jit(solution)/shard_map/psum | solution.py:133
  142.3 252.3 %all-reduce.9.cloned.1.call-start = ((), (), s32[]{:S(2)}) async-start(), calls=%async_computation.3 | async-start | bytes 131072 | tf_op jit(solution)/shard_map/psum | solution.py:135
  266.5 5.0 %copy-start = (f32[32,8,16,256]{3,1,2,0:T(8,128)S(1)}, f32[32,8,16,256]{3,1,2,0:T(8,128)}, u32[]{:S(2)}) copy-start(f32[32,8,16,256]{3,1,2,0:T(8,128)} %copy.46) | copy-start | bytes 12582916
  400.5 57.4 %copy-start.1 = (f32[64,256]{1,0:T(8,128)S(1)}, f32[64,256]{1,0:T(8,128)}, u32[]{:S(2)}) copy-start(f32[64,256]{1,0:T(8,128)} %all-reduce.7.cloned.1.call-done) | copy-start | bytes 196612
  400.5 57.4 %copy-start.2 = (f32[64,256]{1,0:T(8,128)S(1)}, f32[64,256]{1,0:T(8,128)}, u32[]{:S(2)}) copy-start(f32[64,256]{1,0:T(8,128)} %all-reduce.9.cloned.1.call-done) | copy-start | bytes 196612
Sparse Core Ops, SparseCore 0:
  142.4 124.0 all-reduce.6
  276.2 118.3 all-reduce.8
where the time goes:
time: 466 us; the launch traced here: 465 us
  waiting for transfers between devices  317 us (68%)
  blocking collectives  41.3 us (9%)
  starting transfers between devices  30.6 us (7%)
  matrix products  23.7 us (5%)
  other arithmetic  23.2 us (5%)
  local copies, waits for them, and re-layouts  15.3 us (3%)
  between operations  14.4 us (3%)
    psum x2, waiting for transfers between devices, local(): lax.psum(products(columns, flat_basis), ('shift', 'space')) * cell_weight  242 us
    ppermute x4, waiting for transfers between devices, padded_2(): lax.ppermute(tail, axis, [(i, (i + 1) % count) for i in range(ends)])  60.1 us
    psum x1, blocking collectives, local(): lax.psum(products(columns, columns), ('shift', 'space')) * cell_weight  41.3 us
    ppermute x4, starting transfers between devices, padded_2(): lax.ppermute(tail, axis, [(i, (i + 1) % count) for i in range(ends)])  17.2 us
    dot_general x3, matrix products, products(): lax.dot_general(left_side, right_side, (((1,), (1,)), ((), ())), precisio...  12.3 us
    dot_general x2, matrix products, matmul(): return jnp.dot(left_side, right_side, precision=lax.Precision.HIGHEST)  9.82 us
    unnamed x17, local copies, waits for them, and re-layouts  9.58 us
  transfers between devices with their start and end apart: 12, of which 9 were waited for; matrix products, arithmetic and copies ran while one was open for 2% of the time, Pallas kernels for 0%

commit v1 on v0

v1 whole, which is shorter than its diff:
```python
import functools

import jax
import jax.numpy as jnp
from jax import lax
from jax.experimental import pallas as pl
from jax.experimental.pallas import tpu as pltpu
from jax.sharding import PartitionSpec as P

COLS = 8
SWEEPS = 4
GROUP = 8
LOWER_BOUND = 0.1
UPPER_BOUND = 2.0
MESH = pl.DeviceIdType.MESH
HIGH = lax.Precision.HIGHEST


def dot_t(a, b):
    return lax.dot_general(
        a, b, (((1,), (1,)), ((), ())), precision=HIGH, preferred_element_type=jnp.float32
    )


def dot(a, b):
    return lax.dot_general(
        a, b, (((1,), (0,)), ((), ())), precision=HIGH, preferred_element_type=jnp.float32
    )


class Reducer:
    def __init__(self, place, src, first, second, full, sems):
        self.place, self.src, self.first, self.second, self.full = place, src, first, second, full
        self.s1, self.r1, self.s2, self.r2, self.s3, self.r3 = sems
        self.chunk = src.shape[0] // GROUP

    def rows(self, t):
        return pl.ds(pl.multiple_of(t * self.chunk, 8), self.chunk)

    def copy1(self, j):
        t = self.place.member(j)
        return pltpu.make_async_remote_copy(
            self.src.at[self.rows(t)], self.first.at[j - 1], self.s1.at[j - 1], self.r1.at[j - 1],
            device_id=self.place.group_id(t), device_id_type=MESH)

    def copy2(self, j, slot, to):
        return pltpu.make_async_remote_copy(
            self.second.at[slot], self.second.at[slot], self.s2.at[j - 1], self.r2.at[slot],
            device_id=self.place.slab_id(to), device_id_type=MESH)

    def copy3(self, j, owner):
        t = self.place.member(j)
        return pltpu.make_async_remote_copy(
            self.full.at[self.rows(owner)], self.full.at[self.rows(owner)],
            self.s3.at[j - 1], self.r3.at[j - 1],
            device_id=self.place.group_id(t), device_id_type=MESH)

    def start1(self):
        for j in range(1, GROUP):
            self.copy1(j).start()

    def start2(self):
        place = self.place
        total = self.src[self.rows(place.g)]
        for j in range(1, GROUP):
            self.copy1(j).wait_recv()
            total = total + self.first[j - 1]
        self.second[place.z] = total
        for j in range(1, place.slabs):
            self.copy2(j, place.z, lax.rem(place.z + j, place.slabs)).start()

    def start3(self):
        place = self.place
        for j in range(1, place.slabs):
            other = lax.rem(place.z + j, place.slabs)
            self.copy2(j, other, other).wait_recv()
        total = self.second[0]
        for i in range(1, place.slabs):
            total = total + self.second[i]
        self.full[self.rows(place.g)] = total
        for j in range(1, GROUP):
            self.copy3(j, place.g).start()

    def finish(self):
        place = self.place
        for j in range(1, GROUP):
            self.copy3(j, place.member(GROUP - j)).wait_recv()
        for j in range(1, GROUP):
            self.copy1(j).wait_send()
            self.copy3(j, place.g).wait_send()
        for j in range(1, place.slabs):
            self.copy2(j, place.z, lax.rem(place.z + j, place.slabs)).wait_send()


class Place:
    def __init__(self, slabs):
        self.s = lax.axis_index("shift")
        self.p = lax.axis_index("space")
        self.b = lax.rem(self.p, 2)
        self.z = self.p // 2
        self.g = self.s * 2 + self.b
        self.slabs = slabs

    def member(self, j):
        return lax.rem(self.g + j, GROUP)

    def group_id(self, t):
        return (t // 2, self.z * 2 + lax.rem(t, 2))

    def slab_id(self, z):
        return (self.s, z * 2 + self.b)


def kernel(slabs, cell_weight, labels_ref, cond_ref, capa_ref, shift_ref, q_ref,
           out_ref, coef_ref, fac_ref,
           lab, kap, cap, face, dg, rc, rem, sol, dirs, wt, qs, ws,
           gsrc, gfirst, gsecond, gfull, psrc, pfirst, psecond, pfull,
           msrc, mfirst, msecond, mfull, aug,
           lab_s, lab_r, in_s, in_r, out_s, out_r, halo_s, halo_r, loc, gsem, psem, msem):
    place = Place(slabs)
    s, b, z, g = place.s, place.b, place.z, place.g
    new = wt.shape[0]
    basis = q_ref.shape[0]
    cells = q_ref.shape[1] * q_ref.shape[2]
    depth = q_ref.shape[3]
    rows_y = lab.shape[1]

    barrier = pltpu.get_barrier_semaphore()
    for j in range(1, GROUP):
        pl.semaphore_signal(barrier, inc=1, device_id=place.group_id(place.member(j)), device_id_type=MESH)
    for j in range(1, slabs):
        pl.semaphore_signal(barrier, inc=1, device_id=place.slab_id(lax.rem(z + j, slabs)), device_id_type=MESH)
    pl.semaphore_wait(barrier, GROUP - 1 + slabs - 1)

    def tail_part(t):
        return q_ref.at[pl.ds(basis - new + t * COLS, COLS)]

    def slot_in(t):
        return rem.at[:, pl.ds(lax.rem(t, 2) * 2, 2), pl.ds(pl.multiple_of((t // 2) * 8, 8), 8), :]

    def copy_in(j, to, owner):
        return pltpu.make_async_remote_copy(
            tail_part(to), slot_in(owner), in_s.at[j - 1], in_r.at[j - 1],
            device_id=place.group_id(to), device_id_type=MESH)

    pair = lax.rem(b + 1, 2)
    own = lab.at[pl.ds(1 + 2 * b, 2)]
    lab[pl.ds(1 + 2 * b, 2)] = labels_ref[...]
    lab_pair = pltpu.make_async_remote_copy(
        labels_ref, own, lab_s.at[0], lab_r.at[0], device_id=(s, z * 2 + pair), device_id_type=MESH)
    lab_pair.start()

    def edge(ref_src, dst_plane, k, to):
        return pltpu.make_async_remote_copy(
            lab.at[ref_src], lab.at[dst_plane], lab_s.at[k], lab_r.at[k],
            device_id=place.slab_id(to), device_id_type=MESH)

    for j in range(1, GROUP):
        copy_in(j, place.member(j), g).start()
    mine = pltpu.make_async_copy(tail_part(g), slot_in(g), loc.at[0])
    mine.start()

    gsrc[...] = jnp.zeros_like(gsrc)
    for k in range(cells):
        block = q_ref[:, k // 8, k % 8, :]
        qs[k] = block
    @pl.loop(0, cells)
    def _(k):
        block = qs[k]
        gsrc[...] += dot_t(block, block)

    pltpu.make_async_remote_copy(
        labels_ref, lab.at[pl.ds(1 + 2 * pair, 2)], lab_s.at[0], lab_r.at[0],
        device_id=(s, z * 2 + pair), device_id_type=MESH).wait_recv()

    @pl.when(z > 0)
    def _():
        edge(1, 5, 1, z - 1).start()

    @pl.when(z < slabs - 1)
    def _():
        edge(4, 0, 2, z + 1).start()

    @pl.when(z == 0)
    def _():
        lab[0] = jnp.full((rows_y, depth), -1, jnp.int32)
        for n in range(SWEEPS - 1):
            dirs[n, :, 0] = jnp.zeros((COLS, rows_y, depth), jnp.float32)

    @pl.when(z == slabs - 1)
    def _():
        lab[5] = jnp.full((rows_y, depth), -1, jnp.int32)
        for n in range(SWEEPS - 1):
            dirs[n, :, 5] = jnp.zeros((COLS, rows_y, depth), jnp.float32)

    @pl.when(z > 0)
    def _():
        edge(4, 0, 2, z - 1).wait_recv()

    @pl.when(z < slabs - 1)
    def _():
        edge(1, 5, 1, z + 1).wait_recv()

    @pl.loop(0, 6)
    def _(i):
        value = lab[i]
        k_acc = jnp.zeros((rows_y, depth), jnp.float32)
        for m in range(cond_ref.shape[0]):
            k_acc = jnp.where(value == m, cond_ref[m], k_acc)
        kap[i] = k_acc

    shift = shift_ref[g]
    row = lax.broadcasted_iota(jnp.int32, (rows_y, depth), 0)
    lane = lax.broadcasted_iota(jnp.int32, (rows_y, depth), 1)

    @pl.loop(0, 4)
    def _(i):
        value = lab[i + 1]
        c_acc = jnp.zeros((rows_y, depth), jnp.float32)
        for m in range(capa_ref.shape[0]):
            c_acc = jnp.where(value == m, capa_ref[m], c_acc)
        cap[i] = c_acc
        me = kap[i + 1]
        west = 0.5 * (me + kap[i])
        east = 0.5 * (me + kap[i + 2])
        zero = jnp.zeros_like(me)
        k_south = jnp.where(row == 0, zero, pltpu.roll(me, 1, 0))
        k_north = jnp.where(row == rows_y - 1, zero, pltpu.roll(me, rows_y - 1, 0))
        k_below = jnp.where(lane == 0, zero, pltpu.roll(me, 1, 1))
        k_above = jnp.where(lane == depth - 1, zero, pltpu.roll(me, depth - 1, 1))
        south = 0.5 * (me + k_south)
        north = 0.5 * (me + k_north)
        below = 0.5 * (me + k_below)
        above = 0.5 * (me + k_above)
        diag = ((west + east) + (south + north)) + (below + above) + shift * c_acc
        dg[i] = diag
        rc[i] = 1.0 / diag
        face[0, i] = west
        face[1, i] = east
        face[2, i] = jnp.where(row == 0, zero, south)
        face[3, i] = jnp.where(row == rows_y - 1, zero, north)
        face[4, i] = jnp.where(lane == 0, zero, below)
        face[5, i] = jnp.where(lane == depth - 1, zero, above)

    greduce = Reducer(place, gsrc, gfirst, gsecond, gfull, [gsem.at[i] for i in range(6)])

    mine.wait()
    for j in range(1, GROUP):
        copy_in(j, place.member(j), place.member(GROUP - j)).wait_recv()
    greduce.start1()

    center = 0.5 * (UPPER_BOUND + LOWER_BOUND)
    spread = 0.5 * (UPPER_BOUND - LOWER_BOUND)
    ratio = center / spread

    @pl.loop(0, 4)
    def _(i):
        @pl.loop(0, COLS)
        def _(c):
            r = rem[c, i] * cap[i]
            d = (rc[i] * r) / center
            rem[c, i] = r
            sol[c, i] = d
            dirs[0, c, i + 1] = d

    def halo(n, src, dst, k, to):
        return pltpu.make_async_remote_copy(
            dirs.at[n, :, src], dirs.at[n, :, dst], halo_s.at[n, k], halo_r.at[n, k],
            device_id=place.slab_id(to), device_id_type=MESH)

    weight_old = 1.0 / ratio
    for n in range(SWEEPS - 1):
        @pl.when(z > 0)
        def _():
            halo(n, 1, 5, 0, z - 1).start()

        @pl.when(z < slabs - 1)
        def _():
            halo(n, 4, 0, 1, z + 1).start()

        if n == 0:
            greduce.start2()
        if n == 1:
            greduce.start3()
        if n == 2:
            greduce.finish()

        @pl.when(z > 0)
        def _():
            halo(n, 4, 0, 1, z - 1).wait_recv()

        @pl.when(z < slabs - 1)
        def _():
            halo(n, 1, 5, 0, z + 1).wait_recv()

        weight = 1.0 / (2.0 * ratio - weight_old)
        keep, step = weight * weight_old, 2.0 * weight / spread
        weight_old = weight

        @pl.loop(0, 4)
        def _(i):
            @pl.loop(0, COLS)
            def _(c):
                d = dirs[n, c, i + 1]
                near = face[0, i] * dirs[n, c, i] + face[1, i] * dirs[n, c, i + 2]
                near = near + face[2, i] * pltpu.roll(d, 1, 0) + face[3, i] * pltpu.roll(d, rows_y - 1, 0)
                near = near + face[4, i] * pltpu.roll(d, 1, 1) + face[5, i] * pltpu.roll(d, depth - 1, 1)
                r = rem[c, i] - (dg[i] * d - near)
                nd = keep * d + step * (rc[i] * r)
                sol[c, i] = sol[c, i] + nd
                if n + 1 < SWEEPS - 1:
                    rem[c, i] = r
                    dirs[n + 1, c, i + 1] = nd

    def slot_out(t):
        return sol.at[:, pl.ds(lax.rem(t, 2) * 2, 2), pl.ds(pl.multiple_of((t // 2) * 8, 8), 8), :]

    def copy_out(j, to, owner):
        return pltpu.make_async_remote_copy(
            slot_out(to), wt.at[pl.ds(owner * COLS, COLS)], out_s.at[j - 1], out_r.at[j - 1],
            device_id=place.group_id(to), device_id_type=MESH)

    for j in range(1, GROUP):
        copy_out(j, place.member(j), g).start()
    back = pltpu.make_async_copy(slot_out(g), wt.at[pl.ds(g * COLS, COLS)], loc.at[1])
    back.start()

    lab_pair.wait_send()

    @pl.when(z > 0)
    def _():
        edge(1, 5, 1, z - 1).wait_send()
        for n in range(SWEEPS - 1):
            halo(n, 1, 5, 0, z - 1).wait_send()

    @pl.when(z < slabs - 1)
    def _():
        edge(4, 0, 2, z + 1).wait_send()
        for n in range(SWEEPS - 1):
            halo(n, 4, 0, 1, z + 1).wait_send()

    for j in range(1, GROUP):
        copy_in(j, place.member(j), g).wait_send()

    back.wait()
    for j in range(1, GROUP):
        copy_out(j, place.member(j), place.member(GROUP - j)).wait_recv()

    for k in range(cells):
        ws[k] = wt[:, k // 8, k % 8, :]
    psrc[...] = jnp.zeros_like(psrc)
    @pl.loop(0, cells)
    def _(k):
        psrc[...] += dot_t(ws[k], qs[k])
    preduce = Reducer(place, psrc, pfirst, psecond, pfull, [psem.at[i] for i in range(6)])
    preduce.start1()
    preduce.start2()
    preduce.start3()
    for j in range(1, GROUP):
        copy_out(j, place.member(j), g).wait_send()
    preduce.finish()

    proj = pfull[...] * cell_weight
    coef = proj + (proj - dot(proj, gfull[...] * cell_weight))
    coef_ref[...] = coef
    msrc[...] = jnp.zeros_like(msrc)
    @pl.loop(0, cells)
    def _(k):
        w2 = ws[k] - dot(coef_ref[...], qs[k])
        ws[k] = w2
        msrc[...] += dot_t(w2, w2)
    mreduce = Reducer(place, msrc, mfirst, msecond, mfull, [msem.at[i] for i in range(6)])
    mreduce.start1()
    mreduce.start2()
    mreduce.start3()
    mreduce.finish()

    gram = mfull[...] * cell_weight
    r64 = lax.broadcasted_iota(jnp.int32, (new, new), 0)
    c64 = lax.broadcasted_iota(jnp.int32, (new, new), 1)
    eye = jnp.where(r64 == c64, 1.0, 0.0).astype(jnp.float32)
    work = jnp.concatenate([gram, eye], axis=1)
    for j in range(new - 1):
        lo = (j // 8) * 8
        live = work[lo:]
        pivot_row = work[j:j + 1]
        scaled = pivot_row / pivot_row[:, j:j + 1]
        col = live[:, j:j + 1]
        below_pivot = lax.broadcasted_iota(jnp.int32, (new - lo, 1), 0) > (j - lo)
        live = live - jnp.where(below_pivot, col, 0.0) * scaled
        work = jnp.concatenate([work[:lo], live], axis=0) if lo else live
    diag = jnp.sum(jnp.where(r64 == c64, work[:, :new], 0.0), axis=1, keepdims=True)
    work = work / jnp.sqrt(diag)
    upper = jnp.where(c64 >= r64, work[:, :new], 0.0)
    fac_ref[...] = lax.dot_general(
        upper, eye, (((0,), (0,)), ((), ())), precision=HIGH, preferred_element_type=jnp.float32)
    aug[...] = work[:, new:]
    @pl.loop(0, cells)
    def _(k):
        ws[k] = dot(aug[...], ws[k])
    for k in range(cells):
        out_ref[:, k // 8, k % 8, :] = ws[k]


def local(slabs, labels, conductance, capacity_table, shift_values, prior_basis):
    basis, slab_x, quarter, depth = prior_basis.shape
    shifts = shift_values.shape[0]
    new = shifts * COLS
    rows_y = labels.shape[1]
    cells = slab_x * quarter
    count = cells * depth * lax.axis_size("shift") * lax.axis_size("space")
    f32 = jnp.float32

    def reducer(rows, lanes):
        c = rows // GROUP
        return [pltpu.VMEM((rows, lanes), f32), pltpu.VMEM((GROUP - 1, c, lanes), f32),
                pltpu.VMEM((slabs, c, lanes), f32), pltpu.VMEM((rows, lanes), f32)]

    dma = pltpu.SemaphoreType.DMA
    width = max(GROUP, slabs)
    vmem = pl.BlockSpec(memory_space=pltpu.VMEM)
    smem = pl.BlockSpec(memory_space=pltpu.SMEM)
    block, coef, factor = pl.pallas_call(
        functools.partial(kernel, slabs, 1.0 / count),
        out_shape=[
            jax.ShapeDtypeStruct((new, slab_x, quarter, depth), f32),
            jax.ShapeDtypeStruct((new, basis), f32),
            jax.ShapeDtypeStruct((new, new), f32),
        ],
        in_specs=[vmem, smem, smem, smem, vmem],
        out_specs=[vmem] * 3,
        scratch_shapes=[
            pltpu.VMEM((6, rows_y, depth), jnp.int32),
            pltpu.VMEM((6, rows_y, depth), f32),
            pltpu.VMEM((4, rows_y, depth), f32),
            pltpu.VMEM((6, 4, rows_y, depth), f32),
            pltpu.VMEM((4, rows_y, depth), f32),
            pltpu.VMEM((4, rows_y, depth), f32),
            pltpu.VMEM((COLS, 4, rows_y, depth), f32),
            pltpu.VMEM((COLS, 4, rows_y, depth), f32),
            pltpu.VMEM((SWEEPS - 1, COLS, 6, rows_y, depth), f32),
            pltpu.VMEM((new, slab_x, quarter, depth), f32),
            pltpu.VMEM((cells, basis, depth), f32),
            pltpu.VMEM((cells, new, depth), f32),
            *reducer(basis, basis),
            *reducer(new, basis),
            *reducer(new, new),
            pltpu.VMEM((new, new), f32),
            dma((3,)), dma((3,)), dma((GROUP - 1,)), dma((GROUP - 1,)),
            dma((GROUP - 1,)), dma((GROUP - 1,)), dma((SWEEPS - 1, 2)), dma((SWEEPS - 1, 2)),
            dma((2,)), dma((6, width)), dma((6, width)), dma((6, width)),
        ],
        compiler_params=pltpu.CompilerParams(
            collective_id=0, has_side_effects=True, vmem_limit_bytes=48 * 1024 * 1024),
    )(labels, conductance, capacity_table, shift_values, prior_basis)
    return block.reshape(shifts, COLS, slab_x, quarter, depth), coef, factor


def solution(mesh):
    in_specs = (P("space", None, None), P(), P(), P(), P(None, "space", "shift", None))
    out_specs = (P(None, None, "space", "shift", None), P(), P())
    slabs = mesh.shape["space"] // 2
    return jax.shard_map(
        functools.partial(local, slabs), mesh=mesh, in_specs=in_specs, out_specs=out_specs, check_vma=False)
```

time: 466 us -> 117 us (0.25)
  waiting for transfers between devices: 317 us -> 0 us
  Pallas kernels: 0 us -> 109 us
  blocking collectives: 41.3 us -> 0 us
  starting transfers between devices: 30.6 us -> 0 us
  matrix products: 23.7 us -> 0 us
  other arithmetic: 23.2 us -> 0 us
  between operations: 14.4 us -> 0.65 us
  local copies, waits for them, and re-layouts: 15.3 us -> 7.2 us
    psum x2 -> x0, waiting for transfers between devices: 242 us -> none  [local(): lax.psum(products(columns, flat_basis), ('shift', 'space')) * cell_weight]
    pallas_call x0 -> x1, Pallas kernels: none -> 109 us  [local(): pl.pallas_call(functools.partial(kernel, slabs, 1.0 / count), out_shape=[...]
    ppermute x8 -> x0, waiting for transfers between devices: 64.3 us -> none  [the longest x4 60.1 us: padded_2(): lax.ppermute(tail, axis, [(i, (i + 1) % count) for i in range(ends)])]
    psum x1 -> x0, blocking collectives: 41.3 us -> none  [local(): lax.psum(products(columns, columns), ('shift', 'space')) * cell_weight]
    ppermute x8 -> x0, starting transfers between devices: 22.4 us -> none  [the longest x4 17.2 us: padded_2(): lax.ppermute(tail, axis, [(i, (i + 1) % count) for i in range(ends)])]
    dot_general x5 -> x0, matrix products: 22.1 us -> none  [the longest x3 12.3 us: products(): lax.dot_general(left_side, right_side, (((1,), (1,)), ((), ())), precisio...]
    another operation x5 -> x0, other arithmetic: 12.7 us -> none  [the longest x3 6.52 us: local(): factor = jnp.linalg.cholesky(gram_matrix)]
    all_to_all x2 -> x0, waiting for transfers between devices: 10.1 us -> none  [the longest x1 6.27 us: local(): lax.all_to_all(merged, 'shift', split_axis=2, concat_axis=0, tiled=True)]
  transfers between devices with their start and end apart: 12 -> 0, of which waited for: 9 -> 0; matrix products, arithmetic and copies ran while one was open for 2% -> 0% of each run, Pallas kernels for 0% -> 0%
where the time goes in v1:
time: 117 us
  Pallas kernels  109 us (93%)
  local copies, waits for them, and re-layouts  7.2 us (6%)
    pallas_call x1, Pallas kernels, local(): pl.pallas_call(functools.partial(kernel, slabs, 1.0 / count), out_shape=[...  109 us
    unnamed x13, local copies, waits for them, and re-layouts  7.2 us

profile of v1, /device:TPU:0, one launch (start us, length us, event | category | flops | bytes accessed | tf_op | source)
XLA Modules:
  0.0 117.1 jit_solution(11100363843042936084)
XLA Ops:
  0.6 0.0 copy-start
  0.6 2.2 %copy-done = f32[256,2,8,256]{3,2,1,0:T(8,128)S(1)} copy-done((f32[256,2,8,256]{3,2,1,0:T(8,128)S(1)}, f32[256,2,8,256]{3,2,1,0:T(8,128)}, u32[]{:S(2)}) %copy-start) | copy-done | bytes 4194328
  2.8 0.0 copy-start.1
  2.8 0.8 copy-done.1
  3.7 0.0 copy-start.2
  3.7 0.7 copy-done.2
  4.3 0.0 copy-start.3
  4.3 0.7 copy-done.3
  5.0 0.0 copy-start.4
  5.0 0.7 copy-done.4
  5.6 109.3 %shard_map.76 = (f32[64,2,8,256]{3,2,1,0:T(8,128)S(1)}, f32[64,256]{1,0:T(8,128)S(1)}, f32[64,64]{1,0:T(8,128)S(1)}) custom-call(s32[2,32,256]{2,1,0:T(8,128)S(1)} %copy-done.1, f32[8]{0:T(128)S(1)} %copy-done.2, f32[8]{0:T(128)S(1)} %copy-done.3, f32[8]{0:T(128)S(1)} %copy-done.4, f32[256,2,8,256]{3,2,1,0:T(8,128)S(1)} %copy-done), custom_call_target="tpu_custom_call" | custom-call | tf_op jit(solution)/shard_map/pallas_call | solution.py:423
  114.9 1.0 copy.11
  115.9 0.6 copy.12
  116.5 0.6 copy.13
Async XLA Ops:
  0.6 2.2 %copy-start = (f32[256,2,8,256]{3,2,1,0:T(8,128)S(1)}, f32[256,2,8,256]{3,2,1,0:T(8,128)}, u32[]{:S(2)}) copy-start(f32[256,2,8,256]{3,2,1,0:T(8,128)} %q_ref.1) | copy-start | bytes 12582916
  2.8 0.8 copy-start.1
  3.7 0.7 copy-start.2
  4.3 0.7 copy-start.3
  5.0 0.7 copy-start.4

commit v2 on v1

v2 whole, which is shorter than its diff:
```python
import functools

import jax
import jax.numpy as jnp
from jax import lax
from jax.experimental import pallas as pl
from jax.experimental.pallas import tpu as pltpu
from jax.sharding import PartitionSpec as P

COLS = 8
SWEEPS = 4
GROUP = 8
LOWER_BOUND = 0.1
UPPER_BOUND = 2.0
MESH = pl.DeviceIdType.MESH
HIGH = lax.Precision.HIGHEST


def dot(a, b):
    return lax.dot_general(
        a, b, (((1,), (0,)), ((), ())), precision=HIGH, preferred_element_type=jnp.float32
    )


class Reducer:
    def __init__(self, place, src, first, second, full, sems):
        self.place, self.src, self.first, self.second, self.full = place, src, first, second, full
        self.s1, self.r1, self.s2, self.r2, self.s3, self.r3 = sems
        self.chunk = src.shape[0] // GROUP

    def rows(self, t):
        return pl.ds(pl.multiple_of(t * self.chunk, 8), self.chunk)

    def copy1(self, j):
        t = self.place.member(j)
        return pltpu.make_async_remote_copy(
            self.src.at[self.rows(t)], self.first.at[j - 1], self.s1.at[j - 1], self.r1.at[j - 1],
            device_id=self.place.group_id(t), device_id_type=MESH)

    def copy2(self, j, slot, to):
        return pltpu.make_async_remote_copy(
            self.second.at[slot], self.second.at[slot], self.s2.at[j - 1], self.r2.at[slot],
            device_id=self.place.slab_id(to), device_id_type=MESH)

    def copy3(self, j, owner):
        t = self.place.member(j)
        return pltpu.make_async_remote_copy(
            self.full.at[self.rows(owner)], self.full.at[self.rows(owner)],
            self.s3.at[j - 1], self.r3.at[j - 1],
            device_id=self.place.group_id(t), device_id_type=MESH)

    def start1(self):
        for j in range(1, GROUP):
            self.copy1(j).start()

    def start2(self):
        place = self.place
        total = self.src[self.rows(place.g)]
        for j in range(1, GROUP):
            self.copy1(j).wait_recv()
            total = total + self.first[j - 1]
        self.second[place.z] = total
        for j in range(1, place.slabs):
            self.copy2(j, place.z, lax.rem(place.z + j, place.slabs)).start()

    def start3(self):
        place = self.place
        for j in range(1, place.slabs):
            other = lax.rem(place.z + j, place.slabs)
            self.copy2(j, other, other).wait_recv()
        total = self.second[0]
        for i in range(1, place.slabs):
            total = total + self.second[i]
        self.full[self.rows(place.g)] = total
        for j in range(1, GROUP):
            self.copy3(j, place.g).start()

    def finish(self):
        place = self.place
        for j in range(1, GROUP):
            self.copy3(j, place.member(GROUP - j)).wait_recv()
        for j in range(1, GROUP):
            self.copy1(j).wait_send()
            self.copy3(j, place.g).wait_send()
        for j in range(1, place.slabs):
            self.copy2(j, place.z, lax.rem(place.z + j, place.slabs)).wait_send()


class Place:
    def __init__(self, slabs):
        self.s = lax.axis_index("shift")
        self.p = lax.axis_index("space")
        self.b = lax.rem(self.p, 2)
        self.z = self.p // 2
        self.g = self.s * 2 + self.b
        self.slabs = slabs

    def member(self, j):
        return lax.rem(self.g + j, GROUP)

    def group_id(self, t):
        return (t // 2, self.z * 2 + lax.rem(t, 2))

    def slab_id(self, z):
        return (self.s, z * 2 + self.b)


def split(x):
    hi = x.astype(jnp.bfloat16)
    return hi, (x - hi.astype(jnp.float32)).astype(jnp.bfloat16)


def raw(a, b, dims):
    return lax.dot_general(a, b, (dims, ((), ())), preferred_element_type=jnp.float32)


def dot3(a_hi, a_lo, b_hi, b_lo, dims):
    rows = a_hi.shape[0]
    both = raw(jnp.concatenate([a_hi, a_lo], axis=0), b_hi, dims)
    return both[:rows] + (both[rows:] + raw(a_hi, b_lo, dims))


TRANSPOSED = ((1,), (1,))
PLAIN = ((1,), (0,))


def kernel(slabs, cell_weight, labels_hbm, cond_hbm, capa_hbm, shift_hbm, q_hbm,
           out_hbm, coef_ref, fac_ref,
           lab, kap, cap, face, dg, rc, rem, sol, dirs, wt, qs, qh, ql, wh, wl,
           gsrc, gfirst, gsecond, gfull, psrc, pfirst, psecond, pfull,
           msrc, mfirst, msecond, mfull, cross, cond_ref, capa_ref, shift_ref,
           lab_s, lab_r, in_s, in_r, out_s, out_r, halo_s, halo_r, loc, qsem, osem, gsem, psem, msem):
    place = Place(slabs)
    s, b, z, g = place.s, place.b, place.z, place.g
    f32 = jnp.float32
    basis, slab_x, quarter, depth = q_hbm.shape
    new = wt.shape[2]
    cells = slab_x * quarter
    rows_y = lab.shape[1]
    old = basis - new

    def load(k, first, count, i):
        return pltpu.make_async_copy(
            q_hbm.at[pl.ds(first, count), k // quarter, k % quarter, :],
            qs.at[k // quarter, k % quarter, pl.ds(first, count), :], qsem.at[i, k])

    for k in range(cells):
        load(k, old, new, 0).start()
    own_lab = pltpu.make_async_copy(labels_hbm, lab.at[pl.ds(1 + 2 * b, 2)], loc.at[2])
    own_lab.start()
    tables = [pltpu.make_async_copy(src, dst, loc.at[3 + i]) for i, (src, dst) in enumerate(
        [(cond_hbm, cond_ref), (capa_hbm, capa_ref), (shift_hbm, shift_ref)])]
    for copy in tables:
        copy.start()
    for k in range(cells):
        load(k, 0, old, 1).start()

    barrier = pltpu.get_barrier_semaphore()
    for j in range(1, GROUP):
        pl.semaphore_signal(barrier, inc=1, device_id=place.group_id(place.member(j)), device_id_type=MESH)
    for j in range(1, slabs):
        pl.semaphore_signal(barrier, inc=1, device_id=place.slab_id(lax.rem(z + j, slabs)), device_id_type=MESH)
    for n in range(SWEEPS - 1):
        for i in range(1, 5):
            dirs[n, i, 0] = jnp.zeros((COLS, depth), f32)
            dirs[n, i, rows_y + 1] = jnp.zeros((COLS, depth), f32)
    pl.semaphore_wait(barrier, GROUP - 1 + slabs - 1)

    pair = lax.rem(b + 1, 2)

    def lab_pair(owner):
        return pltpu.make_async_remote_copy(
            labels_hbm, lab.at[pl.ds(1 + 2 * owner, 2)], lab_s.at[0], lab_r.at[0],
            device_id=(s, z * 2 + pair), device_id_type=MESH)

    def edge(from_plane, to_plane, k, to):
        return pltpu.make_async_remote_copy(
            lab.at[from_plane], lab.at[to_plane], lab_s.at[k], lab_r.at[k],
            device_id=place.slab_id(to), device_id_type=MESH)

    def slot(field, t):
        return field.at[pl.ds(lax.rem(t, 2) * 2, 2), pl.ds((t // 2) * quarter, quarter)]

    def copy_in(j, to, owner):
        return pltpu.make_async_remote_copy(
            qs.at[:, :, pl.ds(pl.multiple_of(old + to * COLS, COLS), COLS), :], slot(rem, owner),
            in_s.at[j - 1], in_r.at[j - 1], device_id=place.group_id(to), device_id_type=MESH)

    lab_pair(b).start()
    for k in range(cells):
        load(k, old, new, 0).wait()
    for j in range(1, GROUP):
        copy_in(j, place.member(j), g).start()
    mine = pltpu.make_async_copy(
        qs.at[:, :, pl.ds(pl.multiple_of(old + g * COLS, COLS), COLS), :], slot(rem, g), loc.at[0])
    mine.start()
    own_lab.wait()
    lab_pair(pair).wait_recv()

    @pl.when(z > 0)
    def _():
        edge(1, 5, 1, z - 1).start()

    @pl.when(z < slabs - 1)
    def _():
        edge(4, 0, 2, z + 1).start()

    for end, there in ((0, z == 0), (5, z == slabs - 1)):
        @pl.when(there)
        def _():
            lab[end] = jnp.full((rows_y, depth), -1, jnp.int32)
            for n in range(SWEEPS - 1):
                dirs[n, end] = jnp.zeros((rows_y + 2, COLS, depth), f32)

    for k in range(cells):
        load(k, 0, old, 1).wait()
    gsrc[...] = jnp.zeros_like(gsrc)
    cross[...] = jnp.zeros_like(cross)

    @pl.loop(0, cells)
    def _(k):
        hi, lo = split(qs[k // quarter, lax.rem(k, quarter)])
        qh[k] = hi
        ql[k] = lo
        gsrc[...] += raw(hi, hi, TRANSPOSED)
        cross[...] += raw(hi, lo, TRANSPOSED)

    gsrc[...] += cross[...] + cross[...].T

    @pl.when(z > 0)
    def _():
        edge(4, 0, 2, z - 1).wait_recv()

    @pl.when(z < slabs - 1)
    def _():
        edge(1, 5, 1, z + 1).wait_recv()

    for copy in tables:
        copy.wait()

    @pl.loop(0, 6)
    def _(i):
        value = lab[i]
        k_acc = jnp.zeros((rows_y, depth), f32)
        for m in range(cond_ref.shape[0]):
            k_acc = jnp.where(value == m, cond_ref[m], k_acc)
        kap[i] = k_acc

    shift = shift_ref[g]
    row = lax.broadcasted_iota(jnp.int32, (rows_y, depth), 0)
    lane = lax.broadcasted_iota(jnp.int32, (rows_y, depth), 1)

    @pl.loop(0, 4)
    def _(i):
        value = lab[i + 1]
        c_acc = jnp.zeros((rows_y, depth), f32)
        for m in range(capa_ref.shape[0]):
            c_acc = jnp.where(value == m, capa_ref[m], c_acc)
        cap[i] = c_acc
        me = kap[i + 1]
        zero = jnp.zeros_like(me)
        west = 0.5 * (me + kap[i])
        east = 0.5 * (me + kap[i + 2])
        south = 0.5 * (me + jnp.where(row == 0, zero, pltpu.roll(me, 1, 0)))
        north = 0.5 * (me + jnp.where(row == rows_y - 1, zero, pltpu.roll(me, rows_y - 1, 0)))
        below = 0.5 * (me + jnp.where(lane == 0, zero, pltpu.roll(me, 1, 1)))
        above = 0.5 * (me + jnp.where(lane == depth - 1, zero, pltpu.roll(me, depth - 1, 1)))
        diag = ((west + east) + (south + north)) + (below + above) + shift * c_acc
        dg[i] = diag
        rc[i] = 1.0 / diag
        face[0, i] = west
        face[1, i] = east
        face[2, i] = south
        face[3, i] = north
        face[4, i] = jnp.where(lane == 0, zero, below)
        face[5, i] = jnp.where(lane == depth - 1, zero, above)

    greduce = Reducer(place, gsrc, gfirst, gsecond, gfull, [gsem.at[i] for i in range(6)])

    mine.wait()
    for j in range(1, GROUP):
        copy_in(j, place.member(j), place.member(GROUP - j)).wait_recv()
    greduce.start1()

    center = 0.5 * (UPPER_BOUND + LOWER_BOUND)
    spread = 0.5 * (UPPER_BOUND - LOWER_BOUND)
    ratio = center / spread

    def begin(i):
        @pl.loop(0, rows_y // 8)
        def _(t):
            tile = pl.ds(pl.multiple_of(t * 8, 8), 8)
            c_t, rc_t = cap[i, tile], rc[i, tile]
            for u in range(8):
                y = t * 8 + u
                r = rem[i, y] * c_t[u:u + 1]
                d = (rc_t[u:u + 1] * r) / center
                rem[i, y] = r
                sol[i, y] = d
                dirs[0, i + 1, y + 1] = d

    def sweep(n, i, keep, step):
        @pl.loop(0, rows_y // 8)
        def _(t):
            tile = pl.ds(pl.multiple_of(t * 8, 8), 8)
            f = [face[k, i, tile] for k in range(6)]
            dg_t, rc_t = dg[i, tile], rc[i, tile]
            for u in range(8):
                y = t * 8 + u
                w_, e_, s_, n_, b_, a_ = [v[u:u + 1] for v in f]
                d = dirs[n, i + 1, y + 1]
                near = w_ * dirs[n, i, y + 1] + e_ * dirs[n, i + 2, y + 1]
                near = near + s_ * dirs[n, i + 1, y] + n_ * dirs[n, i + 1, y + 2]
                near = near + b_ * pltpu.roll(d, 1, 1) + a_ * pltpu.roll(d, depth - 1, 1)
                r = rem[i, y] - (dg_t[u:u + 1] * d - near)
                nd = keep * d + step * (rc_t[u:u + 1] * r)
                sol[i, y] = sol[i, y] + nd
                if n + 1 < SWEEPS - 1:
                    rem[i, y] = r
                    dirs[n + 1, i + 1, y + 1] = nd

    def halo(n, src, dst, k, to):
        return pltpu.make_async_remote_copy(
            dirs.at[n, src, pl.ds(1, rows_y)], dirs.at[n, dst, pl.ds(1, rows_y)],
            halo_s.at[n, k], halo_r.at[n, k], device_id=place.slab_id(to), device_id_type=MESH)

    def send_halo(n):
        @pl.when(z > 0)
        def _():
            halo(n, 1, 5, 0, z - 1).start()

        @pl.when(z < slabs - 1)
        def _():
            halo(n, 4, 0, 1, z + 1).start()

    begin(0)
    begin(3)
    send_halo(0)
    begin(1)
    begin(2)
    weight_old = 1.0 / ratio
    for n in range(SWEEPS - 1):
        weight = 1.0 / (2.0 * ratio - weight_old)
        keep, step = weight * weight_old, 2.0 * weight / spread
        weight_old = weight
        sweep(n, 1, keep, step)
        sweep(n, 2, keep, step)
        if n == 0:
            greduce.start2()
        if n == 1:
            greduce.start3()
        if n == 2:
            greduce.finish()

        @pl.when(z > 0)
        def _():
            halo(n, 4, 0, 1, z - 1).wait_recv()

        @pl.when(z < slabs - 1)
        def _():
            halo(n, 1, 5, 0, z + 1).wait_recv()

        sweep(n, 0, keep, step)
        sweep(n, 3, keep, step)
        if n + 1 < SWEEPS - 1:
            send_halo(n + 1)

    def copy_out(j, to, owner):
        return pltpu.make_async_remote_copy(
            slot(sol, to), wt.at[:, :, pl.ds(pl.multiple_of(owner * COLS, COLS), COLS), :],
            out_s.at[j - 1], out_r.at[j - 1], device_id=place.group_id(to), device_id_type=MESH)

    for j in range(1, GROUP):
        copy_out(j, place.member(j), g).start()
    back = pltpu.make_async_copy(
        slot(sol, g), wt.at[:, :, pl.ds(pl.multiple_of(g * COLS, COLS), COLS), :], loc.at[1])
    back.start()

    lab_pair(b).wait_send()

    @pl.when(z > 0)
    def _():
        edge(1, 5, 1, z - 1).wait_send()
        for n in range(SWEEPS - 1):
            halo(n, 1, 5, 0, z - 1).wait_send()

    @pl.when(z < slabs - 1)
    def _():
        edge(4, 0, 2, z + 1).wait_send()
        for n in range(SWEEPS - 1):
            halo(n, 4, 0, 1, z + 1).wait_send()

    for j in range(1, GROUP):
        copy_in(j, place.member(j), g).wait_send()
    psrc[...] = jnp.zeros_like(psrc)
    msrc[...] = jnp.zeros_like(msrc)
    back.wait()
    for j in range(1, GROUP):
        copy_out(j, place.member(j), place.member(GROUP - j)).wait_recv()

    @pl.loop(0, cells // 4)
    def _(k4):
        total = psrc[...]
        for i in range(4):
            k = k4 * 4 + i
            hi, lo = split(wt[k // quarter, lax.rem(k, quarter)])
            total = total + dot3(hi, lo, qh[k], ql[k], TRANSPOSED)
        psrc[...] = total

    preduce = Reducer(place, psrc, pfirst, psecond, pfull, [psem.at[i] for i in range(6)])
    preduce.start1()
    preduce.start2()
    preduce.start3()
    for j in range(1, GROUP):
        copy_out(j, place.member(j), g).wait_send()
    preduce.finish()

    proj = pfull[...] * cell_weight
    coef = proj + (proj - dot(proj, gfull[...] * cell_weight))
    coef_ref[...] = coef
    coef_hi, coef_lo = split(coef)
    qs_new = pl.ds(0, new)

    @pl.loop(0, cells // 4)
    def _(k4):
        same = msrc[...]
        mixed = cross[qs_new, qs_new] * jnp.where(k4 == 0, 0.0, 1.0)
        for i in range(4):
            k = k4 * 4 + i
            w2 = wt[k // quarter, lax.rem(k, quarter)] - dot3(coef_hi, coef_lo, qh[k], ql[k], PLAIN)
            hi, lo = split(w2)
            wh[k] = hi
            wl[k] = lo
            same = same + raw(hi, hi, TRANSPOSED)
            mixed = mixed + raw(hi, lo, TRANSPOSED)
        msrc[...] = same
        cross[qs_new, qs_new] = mixed

    mixed = cross[qs_new, qs_new]
    msrc[...] += mixed + mixed.T
    mreduce = Reducer(place, msrc, mfirst, msecond, mfull, [msem.at[i] for i in range(6)])
    mreduce.start1()
    mreduce.start2()
    mreduce.start3()
    mreduce.finish()

    gram = mfull[...] * cell_weight
    r64 = lax.broadcasted_iota(jnp.int32, (new, new), 0)
    c64 = lax.broadcasted_iota(jnp.int32, (new, new), 1)
    eye = jnp.where(r64 == c64, 1.0, 0.0).astype(f32)
    work = jnp.concatenate([gram, eye], axis=1)
    for j in range(new - 1):
        lo = (j // 8) * 8
        live = work[lo:]
        pivot_row = work[j:j + 1]
        scaled = pivot_row / pivot_row[:, j:j + 1]
        col = live[:, j:j + 1]
        below_pivot = lax.broadcasted_iota(jnp.int32, (new - lo, 1), 0) > (j - lo)
        live = live - jnp.where(below_pivot, col, 0.0) * scaled
        work = jnp.concatenate([work[:lo], live], axis=0) if lo else live
    diag = jnp.sum(jnp.where(r64 == c64, work[:, :new], 0.0), axis=1, keepdims=True)
    work = work / jnp.sqrt(diag)
    upper = jnp.where(c64 >= r64, work[:, :new], 0.0)
    fac_ref[...] = lax.dot_general(
        upper, eye, (((0,), (0,)), ((), ())), precision=HIGH, preferred_element_type=f32)
    inv_hi, inv_lo = split(work[:, new:])

    def result(k):
        return pltpu.make_async_copy(
            wt.at[k // quarter, k % quarter], out_hbm.at[:, k // quarter, k % quarter, :], osem.at[k])

    for k in range(cells):
        wt[k // quarter, k % quarter] = dot3(inv_hi, inv_lo, wh[k], wl[k], PLAIN)
        result(k).start()
    for k in range(cells):
        result(k).wait()


def local(slabs, labels, conductance, capacity_table, shift_values, prior_basis):
    basis, slab_x, quarter, depth = prior_basis.shape
    shifts = shift_values.shape[0]
    new = shifts * COLS
    rows_y = labels.shape[1]
    cells = slab_x * quarter
    count = cells * depth * lax.axis_size("shift") * lax.axis_size("space")
    f32 = jnp.float32

    def reducer(rows, lanes):
        c = rows // GROUP
        return [pltpu.VMEM((rows, lanes), f32), pltpu.VMEM((GROUP - 1, c, lanes), f32),
                pltpu.VMEM((slabs, c, lanes), f32), pltpu.VMEM((rows, lanes), f32)]

    dma = pltpu.SemaphoreType.DMA
    width = max(GROUP, slabs)
    vmem = pl.BlockSpec(memory_space=pltpu.VMEM)
    block, coef, factor = pl.pallas_call(
        functools.partial(kernel, slabs, 1.0 / count),
        out_shape=[
            jax.ShapeDtypeStruct((new, slab_x, quarter, depth), f32),
            jax.ShapeDtypeStruct((new, basis), f32),
            jax.ShapeDtypeStruct((new, new), f32),
        ],
        in_specs=[pl.BlockSpec(memory_space=pl.ANY)] * 5,
        out_specs=[pl.BlockSpec(memory_space=pl.ANY), vmem, vmem],
        scratch_shapes=[
            pltpu.VMEM((6, rows_y, depth), jnp.int32),
            pltpu.VMEM((6, rows_y, depth), f32),
            pltpu.VMEM((4, rows_y, depth), f32),
            pltpu.VMEM((6, 4, rows_y, depth), f32),
            pltpu.VMEM((4, rows_y, depth), f32),
            pltpu.VMEM((4, rows_y, depth), f32),
            pltpu.VMEM((4, rows_y, COLS, depth), f32),
            pltpu.VMEM((4, rows_y, COLS, depth), f32),
            pltpu.VMEM((SWEEPS - 1, 6, rows_y + 2, COLS, depth), f32),
            pltpu.VMEM((slab_x, quarter, new, depth), f32),
            pltpu.VMEM((slab_x, quarter, basis, depth), f32),
            pltpu.VMEM((cells, basis, depth), jnp.bfloat16),
            pltpu.VMEM((cells, basis, depth), jnp.bfloat16),
            pltpu.VMEM((cells, new, depth), jnp.bfloat16),
            pltpu.VMEM((cells, new, depth), jnp.bfloat16),
            *reducer(basis, basis),
            *reducer(new, basis),
            *reducer(new, new),
            pltpu.VMEM((basis, basis), f32),
            pltpu.SMEM(conductance.shape, f32),
            pltpu.SMEM(capacity_table.shape, f32),
            pltpu.SMEM(shift_values.shape, f32),
            dma((3,)), dma((3,)), dma((GROUP - 1,)), dma((GROUP - 1,)),
            dma((GROUP - 1,)), dma((GROUP - 1,)), dma((SWEEPS - 1, 2)), dma((SWEEPS - 1, 2)),
            dma((6,)), dma((2, cells)), dma((cells,)),
            dma((6, width)), dma((6, width)), dma((6, width)),
        ],
        compiler_params=pltpu.CompilerParams(
            collective_id=0, has_side_effects=True, vmem_limit_bytes=48 * 1024 * 1024),
    )(labels, conductance, capacity_table, shift_values, prior_basis)
    return block.reshape(shifts, COLS, slab_x, quarter, depth), coef, factor


def solution(mesh):
    in_specs = (P("space", None, None), P(), P(), P(), P(None, "space", "shift", None))
    out_specs = (P(None, None, "space", "shift", None), P(), P())
    slabs = mesh.shape["space"] // 2
    return jax.shard_map(
        functools.partial(local, slabs), mesh=mesh, in_specs=in_specs, out_specs=out_specs, check_vma=False)
```

time: 117 us -> 103 us (0.88)
  Pallas kernels: 109 us -> 95.3 us
    pallas_call x1, Pallas kernels: 109 us -> 95.3 us  [local(): pl.pallas_call(functools.partial(kernel, slabs, 1.0 / count), out_shape=[...]
where the time goes in v2:
time: 103 us
  Pallas kernels  95.3 us (93%)
  local copies, waits for them, and re-layouts  7.2 us (7%)
    pallas_call x1, Pallas kernels, local(): pl.pallas_call(functools.partial(kernel, slabs, 1.0 / count), out_shape=[...  95.3 us
    unnamed x13, local copies, waits for them, and re-layouts  7.2 us

profile of v2, /device:TPU:0, one launch (start us, length us, event | category | flops | bytes accessed | tf_op | source)
XLA Modules:
  0.0 103.1 jit_solution(4869090664437833044)
XLA Ops:
  0.6 0.0 copy-start
  0.6 2.2 %copy-done = f32[256,2,8,256]{3,2,1,0:T(8,128)S(1)} copy-done((f32[256,2,8,256]{3,2,1,0:T(8,128)S(1)}, f32[256,2,8,256]{3,2,1,0:T(8,128)}, u32[]{:S(2)}) %copy-start) | copy-done | bytes 4194328
  2.8 0.0 copy-start.1
  2.8 0.8 copy-done.1
  3.7 0.0 copy-start.2
  3.7 0.7 copy-done.2
  4.3 0.0 copy-start.3
  4.3 0.7 copy-done.3
  5.0 0.0 copy-start.4
  5.0 0.7 copy-done.4
  5.6 95.3 %shard_map.76 = (f32[64,2,8,256]{3,2,1,0:T(8,128)S(1)}, f32[64,256]{1,0:T(8,128)S(1)}, f32[64,64]{1,0:T(8,128)S(1)}) custom-call(s32[2,32,256]{2,1,0:T(8,128)S(1)} %copy-done.1, f32[8]{0:T(128)S(1)} %copy-done.2, f32[8]{0:T(128)S(1)} %copy-done.3, f32[8]{0:T(128)S(1)} %copy-done.4, f32[256,2,8,256]{3,2,1,0:T(8,128)S(1)} %copy-done), custom_call_target="tpu_custom_call" | custom-call | tf_op jit(solution)/shard_map/pallas_call | solution.py:496
  100.9 1.0 copy.11
  101.9 0.6 copy.12
  102.5 0.6 copy.13
Async XLA Ops:
  0.6 2.2 %copy-start = (f32[256,2,8,256]{3,2,1,0:T(8,128)S(1)}, f32[256,2,8,256]{3,2,1,0:T(8,128)}, u32[]{:S(2)}) copy-start(f32[256,2,8,256]{3,2,1,0:T(8,128)} %q_hbm.1) | copy-start | bytes 12582916
  2.8 0.8 copy-start.1
  3.7 0.7 copy-start.2
  4.3 0.7 copy-start.3
  5.0 0.7 copy-start.4

commit v3 on v2

--- a/solution.py
+++ b/solution.py
@@ -125,11 +125,11 @@
 
 
 def kernel(slabs, cell_weight, labels_hbm, cond_hbm, capa_hbm, shift_hbm, q_hbm,
-           out_hbm, coef_ref, fac_ref,
-           lab, kap, cap, face, dg, rc, rem, sol, dirs, wt, qs, qh, ql, wh, wl,
+           out_ref, coef_ref, fac_ref,
+           lab, kap, cap, face, dg, rc, rem, sol, dirs, wt, qn, qs, qh, ql, wh, wl,
            gsrc, gfirst, gsecond, gfull, psrc, pfirst, psecond, pfull,
-           msrc, mfirst, msecond, mfull, cross, cond_ref, capa_ref, shift_ref,
-           lab_s, lab_r, in_s, in_r, out_s, out_r, halo_s, halo_r, loc, qsem, osem, gsem, psem, msem):
+           cross, cond_ref, capa_ref, shift_ref,
+           lab_s, lab_r, in_s, in_r, out_s, out_r, halo_s, halo_r, loc, qsem, osem, gsem, psem):
     place = Place(slabs)
     s, b, z, g = place.s, place.b, place.z, place.g
     f32 = jnp.float32
@@ -141,19 +141,22 @@
 
     def load(k, first, count, i):
         return pltpu.make_async_copy(
-            q_hbm.at[pl.ds(first, count), k // quarter, k % quarter, :],
+            qn.at[pl.ds(first, count), k // quarter, k % quarter, :],
             qs.at[k // quarter, k % quarter, pl.ds(first, count), :], qsem.at[i, k])
 
-    for k in range(cells):
-        load(k, old, new, 0).start()
+    fetch = [pltpu.make_async_copy(q_hbm.at[pl.ds(first, count)], qn.at[pl.ds(first, count)], loc.at[6 + i])
+             for i, (first, count) in enumerate([(old, new), (0, old)])]
+    fetch[0].start()
     own_lab = pltpu.make_async_copy(labels_hbm, lab.at[pl.ds(1 + 2 * b, 2)], loc.at[2])
     own_lab.start()
     tables = [pltpu.make_async_copy(src, dst, loc.at[3 + i]) for i, (src, dst) in enumerate(
         [(cond_hbm, cond_ref), (capa_hbm, capa_ref), (shift_hbm, shift_ref)])]
     for copy in tables:
         copy.start()
-    for k in range(cells):
-        load(k, 0, old, 1).start()
+    fetch[1].start()
+    fetch[0].wait()
+    for k in range(cells):
+        load(k, old, new, 0).start()
 
     barrier = pltpu.get_barrier_semaphore()
     for j in range(1, GROUP):
@@ -194,6 +197,9 @@
     mine = pltpu.make_async_copy(
         qs.at[:, :, pl.ds(pl.multiple_of(old + g * COLS, COLS), COLS), :], slot(rem, g), loc.at[0])
     mine.start()
+    fetch[1].wait()
+    for k in range(cells):
+        load(k, 0, old, 1).start()
     own_lab.wait()
     lab_pair(pair).wait_recv()
 
@@ -393,19 +399,23 @@
     for j in range(1, GROUP):
         copy_in(j, place.member(j), g).wait_send()
     psrc[...] = jnp.zeros_like(psrc)
-    msrc[...] = jnp.zeros_like(msrc)
     back.wait()
     for j in range(1, GROUP):
         copy_out(j, place.member(j), place.member(GROUP - j)).wait_recv()
 
     @pl.loop(0, cells // 4)
     def _(k4):
-        total = psrc[...]
+        total = psrc[:, :basis]
+        same = psrc[:, basis:basis + new]
         for i in range(4):
             k = k4 * 4 + i
-            hi, lo = split(wt[k // quarter, lax.rem(k, quarter)])
+            w = wt[k // quarter, lax.rem(k, quarter)]
+            hi, lo = split(w)
             total = total + dot3(hi, lo, qh[k], ql[k], TRANSPOSED)
-        psrc[...] = total
+            same = same + lax.dot_general(
+                w, w, (TRANSPOSED, ((), ())), precision=HIGH, preferred_element_type=f32)
+        psrc[:, :basis] = total
+        psrc[:, basis:basis + new] = same
 
     preduce = Reducer(place, psrc, pfirst, psecond, pfull, [psem.at[i] for i in range(6)])
     preduce.start1()
@@ -415,49 +425,34 @@
         copy_out(j, place.member(j), g).wait_send()
     preduce.finish()
 
-    proj = pfull[...] * cell_weight
-    coef = proj + (proj - dot(proj, gfull[...] * cell_weight))
+    proj = pfull[:, :basis] * cell_weight
+    own_gram = pfull[:, basis:basis + new] * cell_weight
+    basis_gram = gfull[...] * cell_weight
+    coef = proj + (proj - dot(proj, basis_gram))
     coef_ref[...] = coef
     coef_hi, coef_lo = split(coef)
-    qs_new = pl.ds(0, new)
-
-    @pl.loop(0, cells // 4)
-    def _(k4):
-        same = msrc[...]
-        mixed = cross[qs_new, qs_new] * jnp.where(k4 == 0, 0.0, 1.0)
-        for i in range(4):
-            k = k4 * 4 + i
-            w2 = wt[k // quarter, lax.rem(k, quarter)] - dot3(coef_hi, coef_lo, qh[k], ql[k], PLAIN)
-            hi, lo = split(w2)
-            wh[k] = hi
-            wl[k] = lo
-            same = same + raw(hi, hi, TRANSPOSED)
-            mixed = mixed + raw(hi, lo, TRANSPOSED)
-        msrc[...] = same
-        cross[qs_new, qs_new] = mixed
-
-    mixed = cross[qs_new, qs_new]
-    msrc[...] += mixed + mixed.T
-    mreduce = Reducer(place, msrc, mfirst, msecond, mfull, [msem.at[i] for i in range(6)])
-    mreduce.start1()
-    mreduce.start2()
-    mreduce.start3()
-    mreduce.finish()
-
-    gram = mfull[...] * cell_weight
+
+    half = dot(coef, basis_gram) * 0.5 - proj
+    turn = lax.dot_general(coef, half, (TRANSPOSED, ((), ())), precision=HIGH, preferred_element_type=f32)
+    gram = own_gram + (turn + turn.T)
+
     r64 = lax.broadcasted_iota(jnp.int32, (new, new), 0)
     c64 = lax.broadcasted_iota(jnp.int32, (new, new), 1)
     eye = jnp.where(r64 == c64, 1.0, 0.0).astype(f32)
     work = jnp.concatenate([gram, eye], axis=1)
-    for j in range(new - 1):
-        lo = (j // 8) * 8
-        live = work[lo:]
-        pivot_row = work[j:j + 1]
-        scaled = pivot_row / pivot_row[:, j:j + 1]
-        col = live[:, j:j + 1]
-        below_pivot = lax.broadcasted_iota(jnp.int32, (new - lo, 1), 0) > (j - lo)
-        live = live - jnp.where(below_pivot, col, 0.0) * scaled
-        work = jnp.concatenate([work[:lo], live], axis=0) if lo else live
+    per = new // cells
+    for k in range(cells):
+        for j in range(k * per, min((k + 1) * per, new - 1)):
+            lo = (j // 8) * 8
+            live = work[lo:]
+            pivot_row = work[j:j + 1]
+            scaled = pivot_row / pivot_row[:, j:j + 1]
+            col = live[:, j:j + 1]
+            below_pivot = lax.broadcasted_iota(jnp.int32, (new - lo, 1), 0) > (j - lo)
+            live = live - jnp.where(below_pivot, col, 0.0) * scaled
+            work = jnp.concatenate([work[:lo], live], axis=0) if lo else live
+        w2 = wt[k // quarter, k % quarter] - dot3(coef_hi, coef_lo, qh[k], ql[k], PLAIN)
+        wh[k], wl[k] = split(w2)
     diag = jnp.sum(jnp.where(r64 == c64, work[:, :new], 0.0), axis=1, keepdims=True)
     work = work / jnp.sqrt(diag)
     upper = jnp.where(c64 >= r64, work[:, :new], 0.0)
@@ -467,7 +462,7 @@
 
     def result(k):
         return pltpu.make_async_copy(
-            wt.at[k // quarter, k % quarter], out_hbm.at[:, k // quarter, k % quarter, :], osem.at[k])
+            wt.at[k // quarter, k % quarter], out_ref.at[:, k // quarter, k % quarter, :], osem.at[k])
 
     for k in range(cells):
         wt[k // quarter, k % quarter] = dot3(inv_hi, inv_lo, wh[k], wl[k], PLAIN)
@@ -500,8 +495,8 @@
             jax.ShapeDtypeStruct((new, basis), f32),
             jax.ShapeDtypeStruct((new, new), f32),
         ],
-        in_specs=[pl.BlockSpec(memory_space=pl.ANY)] * 5,
-        out_specs=[pl.BlockSpec(memory_space=pl.ANY), vmem, vmem],
+        in_specs=[pl.BlockSpec(memory_space=pltpu.HBM)] * 5,
+        out_specs=[vmem] * 3,
         scratch_shapes=[
             pltpu.VMEM((6, rows_y, depth), jnp.int32),
             pltpu.VMEM((6, rows_y, depth), f32),
@@ -513,22 +508,22 @@
             pltpu.VMEM((4, rows_y, COLS, depth), f32),
             pltpu.VMEM((SWEEPS - 1, 6, rows_y + 2, COLS, depth), f32),
             pltpu.VMEM((slab_x, quarter, new, depth), f32),
+            pltpu.VMEM((basis, slab_x, quarter, depth), f32),
             pltpu.VMEM((slab_x, quarter, basis, depth), f32),
             pltpu.VMEM((cells, basis, depth), jnp.bfloat16),
             pltpu.VMEM((cells, basis, depth), jnp.bfloat16),
             pltpu.VMEM((cells, new, depth), jnp.bfloat16),
             pltpu.VMEM((cells, new, depth), jnp.bfloat16),
             *reducer(basis, basis),
-            *reducer(new, basis),
-            *reducer(new, new),
+            *reducer(new, basis + 128),
             pltpu.VMEM((basis, basis), f32),
             pltpu.SMEM(conductance.shape, f32),
             pltpu.SMEM(capacity_table.shape, f32),
             pltpu.SMEM(shift_values.shape, f32),
             dma((3,)), dma((3,)), dma((GROUP - 1,)), dma((GROUP - 1,)),
             dma((GROUP - 1,)), dma((GROUP - 1,)), dma((SWEEPS - 1, 2)), dma((SWEEPS - 1, 2)),
-            dma((6,)), dma((2, cells)), dma((cells,)),
-            dma((6, width)), dma((6, width)), dma((6, width)),
+            dma((8,)), dma((2, cells)), dma((cells,)),
+            dma((6, width)), dma((6, width)),
         ],
         compiler_params=pltpu.CompilerParams(
             collective_id=0, has_side_effects=True, vmem_limit_bytes=48 * 1024 * 1024),

time: 103 us -> 90.5 us (0.88)
  Pallas kernels: 95.3 us -> 82.4 us
    pallas_call x1, Pallas kernels: 95.3 us -> 82.4 us  [local(): pl.pallas_call(functools.partial(kernel, slabs, 1.0 / count), out_shape=[...]
where the time goes in v3:
time: 90.5 us; the launch traced here: 90.2 us
  Pallas kernels  82.4 us (91%)
  local copies, waits for them, and re-layouts  7.2 us (8%)
    pallas_call x1, Pallas kernels, local(): pl.pallas_call(functools.partial(kernel, slabs, 1.0 / count), out_shape=[...  82.4 us
    unnamed x13, local copies, waits for them, and re-layouts  7.2 us

profile of v3, /device:TPU:0, one launch (start us, length us, event | category | flops | bytes accessed | tf_op | source)
XLA Modules:
  0.0 90.2 jit_solution(3360720453942992163)
XLA Ops:
  0.6 0.0 copy-start
  0.6 2.2 %copy-done = f32[256,2,8,256]{3,2,1,0:T(8,128)S(1)} copy-done((f32[256,2,8,256]{3,2,1,0:T(8,128)S(1)}, f32[256,2,8,256]{3,2,1,0:T(8,128)}, u32[]{:S(2)}) %copy-start) | copy-done | bytes 4194328
  2.8 0.0 copy-start.1
  2.8 0.8 copy-done.1
  3.7 0.0 copy-start.2
  3.7 0.7 copy-done.2
  4.3 0.0 copy-start.3
  4.3 0.7 copy-done.3
  5.0 0.0 copy-start.4
  5.0 0.7 copy-done.4
  5.6 82.4 %shard_map.76 = (f32[64,2,8,256]{3,2,1,0:T(8,128)S(1)}, f32[64,256]{1,0:T(8,128)S(1)}, f32[64,64]{1,0:T(8,128)S(1)}) custom-call(s32[2,32,256]{2,1,0:T(8,128)S(1)} %copy-done.1, f32[8]{0:T(128)S(1)} %copy-done.2, f32[8]{0:T(128)S(1)} %copy-done.3, f32[8]{0:T(128)S(1)} %copy-done.4, f32[256,2,8,256]{3,2,1,0:T(8,128)S(1)} %copy-done), custom_call_target="tpu_custom_call" | custom-call | tf_op jit(solution)/shard_map/pallas_call | solution.py:491
  88.0 1.0 %copy.11 = f32[8,8,2,8,256]{4,3,2,1,0:T(8,128)} copy(f32[8,8,2,8,256]{4,3,2,1,0:T(8,128)S(1)} %bitcast.1) | data formatting | bytes 2097152
  89.0 0.6 copy.12
  89.6 0.6 copy.13
Async XLA Ops:
  0.6 2.2 %copy-start = (f32[256,2,8,256]{3,2,1,0:T(8,128)S(1)}, f32[256,2,8,256]{3,2,1,0:T(8,128)}, u32[]{:S(2)}) copy-start(f32[256,2,8,256]{3,2,1,0:T(8,128)} %q_hbm.1) | copy-start | bytes 12582916
  2.8 0.8 copy-start.1
  3.7 0.7 copy-start.2
  4.3 0.7 copy-start.3
  5.0 0.7 copy-start.4

commit v4 on v3

--- a/solution.py
+++ b/solution.py
@@ -181,22 +181,33 @@
             lab.at[from_plane], lab.at[to_plane], lab_s.at[k], lab_r.at[k],
             device_id=place.slab_id(to), device_id_type=MESH)
 
-    def slot(field, t):
-        return field.at[pl.ds(lax.rem(t, 2) * 2, 2), pl.ds((t // 2) * quarter, quarter)]
-
-    def copy_in(j, to, owner):
-        return pltpu.make_async_remote_copy(
-            qs.at[:, :, pl.ds(pl.multiple_of(old + to * COLS, COLS), COLS), :], slot(rem, owner),
-            in_s.at[j - 1], in_r.at[j - 1], device_id=place.group_id(to), device_id_type=MESH)
+    def plane_of(member_b, part):
+        return member_b if part == 0 else 1 - member_b
+
+    def column(t):
+        return pl.ds(pl.multiple_of(t * COLS, COLS), COLS)
+
+    def slot(field, t, part):
+        tb = lax.rem(t, 2)
+        return field.at[2 * tb + plane_of(tb, part), pl.ds((t // 2) * quarter, quarter)]
+
+    def tail(t, part):
+        return qs.at[plane_of(b, part), :, pl.ds(pl.multiple_of(old + t * COLS, COLS), COLS), :]
+
+    def copy_in(j, to, owner, part):
+        return pltpu.make_async_remote_copy(
+            tail(to, part), slot(rem, owner, part), in_s.at[part, j - 1], in_r.at[part, j - 1],
+            device_id=place.group_id(to), device_id_type=MESH)
 
     lab_pair(b).start()
     for k in range(cells):
         load(k, old, new, 0).wait()
-    for j in range(1, GROUP):
-        copy_in(j, place.member(j), g).start()
-    mine = pltpu.make_async_copy(
-        qs.at[:, :, pl.ds(pl.multiple_of(old + g * COLS, COLS), COLS), :], slot(rem, g), loc.at[0])
-    mine.start()
+    for part in (0, 1):
+        for j in range(1, GROUP):
+            copy_in(j, place.member(j), g, part).start()
+    mine = [pltpu.make_async_copy(tail(g, part), slot(rem, g, part), loc.at[8 * part]) for part in (0, 1)]
+    for copy in mine:
+        copy.start()
     fetch[1].wait()
     for k in range(cells):
         load(k, 0, old, 1).start()
@@ -283,10 +294,10 @@
 
     greduce = Reducer(place, gsrc, gfirst, gsecond, gfull, [gsem.at[i] for i in range(6)])
 
-    mine.wait()
-    for j in range(1, GROUP):
-        copy_in(j, place.member(j), place.member(GROUP - j)).wait_recv()
-    greduce.start1()
+    def arrived(part):
+        mine[part].wait()
+        for j in range(1, GROUP):
+            copy_in(j, place.member(j), place.member(GROUP - j), part).wait_recv()
 
     center = 0.5 * (UPPER_BOUND + LOWER_BOUND)
     spread = 0.5 * (UPPER_BOUND - LOWER_BOUND)
@@ -339,11 +350,29 @@
         def _():
             halo(n, 4, 0, 1, z + 1).start()
 
+    arrived(0)
     begin(0)
     begin(3)
     send_halo(0)
+    arrived(1)
+    greduce.start1()
     begin(1)
     begin(2)
+    def copy_out(j, to, owner, part, reader_b):
+        return pltpu.make_async_remote_copy(
+            slot(sol, to, part), wt.at[plane_of(reader_b, part), :, column(owner), :],
+            out_s.at[part, j - 1], out_r.at[part, j - 1],
+            device_id=place.group_id(to), device_id_type=MESH)
+
+    back = [pltpu.make_async_copy(
+        slot(sol, g, part), wt.at[plane_of(b, part), :, column(g), :], loc.at[1 + 8 * part]) for part in (0, 1)]
+
+    def send_out(part):
+        for j in range(1, GROUP):
+            to = place.member(j)
+            copy_out(j, to, g, part, lax.rem(to, 2)).start()
+        back[part].start()
+
     weight_old = 1.0 / ratio
     for n in range(SWEEPS - 1):
         weight = 1.0 / (2.0 * ratio - weight_old)
@@ -351,6 +380,8 @@
         weight_old = weight
         sweep(n, 1, keep, step)
         sweep(n, 2, keep, step)
+        if n == SWEEPS - 2:
+            send_out(1)
         if n == 0:
             greduce.start2()
         if n == 1:
@@ -371,16 +402,7 @@
         if n + 1 < SWEEPS - 1:
             send_halo(n + 1)
 
-    def copy_out(j, to, owner):
-        return pltpu.make_async_remote_copy(
-            slot(sol, to), wt.at[:, :, pl.ds(pl.multiple_of(owner * COLS, COLS), COLS), :],
-            out_s.at[j - 1], out_r.at[j - 1], device_id=place.group_id(to), device_id_type=MESH)
-
-    for j in range(1, GROUP):
-        copy_out(j, place.member(j), g).start()
-    back = pltpu.make_async_copy(
-        slot(sol, g), wt.at[:, :, pl.ds(pl.multiple_of(g * COLS, COLS), COLS), :], loc.at[1])
-    back.start()
+    send_out(0)
 
     lab_pair(b).wait_send()
 
@@ -396,33 +418,39 @@
         for n in range(SWEEPS - 1):
             halo(n, 4, 0, 1, z + 1).wait_send()
 
-    for j in range(1, GROUP):
-        copy_in(j, place.member(j), g).wait_send()
+    for part in (0, 1):
+        for j in range(1, GROUP):
+            copy_in(j, place.member(j), g, part).wait_send()
     psrc[...] = jnp.zeros_like(psrc)
-    back.wait()
-    for j in range(1, GROUP):
-        copy_out(j, place.member(j), place.member(GROUP - j)).wait_recv()
-
-    @pl.loop(0, cells // 4)
-    def _(k4):
-        total = psrc[:, :basis]
-        same = psrc[:, basis:basis + new]
-        for i in range(4):
-            k = k4 * 4 + i
-            w = wt[k // quarter, lax.rem(k, quarter)]
-            hi, lo = split(w)
-            total = total + dot3(hi, lo, qh[k], ql[k], TRANSPOSED)
-            same = same + lax.dot_general(
-                w, w, (TRANSPOSED, ((), ())), precision=HIGH, preferred_element_type=f32)
-        psrc[:, :basis] = total
-        psrc[:, basis:basis + new] = same
+    for part in (1, 0):
+        back[part].wait()
+        for j in range(1, GROUP):
+            copy_out(j, place.member(j), place.member(GROUP - j), part, b).wait_recv()
+        plane = plane_of(b, part)
+
+        @pl.loop(0, quarter // 4)
+        def _(k4):
+            total = psrc[:, :basis]
+            same = psrc[:, basis:basis + new]
+            for i in range(4):
+                y = k4 * 4 + i
+                k = plane * quarter + y
+                w = wt[plane, y]
+                hi, lo = split(w)
+                total = total + dot3(hi, lo, qh[k], ql[k], TRANSPOSED)
+                same = same + lax.dot_general(
+                    w, w, (TRANSPOSED, ((), ())), precision=HIGH, preferred_element_type=f32)
+            psrc[:, :basis] = total
+            psrc[:, basis:basis + new] = same
 
     preduce = Reducer(place, psrc, pfirst, psecond, pfull, [psem.at[i] for i in range(6)])
     preduce.start1()
     preduce.start2()
     preduce.start3()
-    for j in range(1, GROUP):
-        copy_out(j, place.member(j), g).wait_send()
+    for part in (0, 1):
+        for j in range(1, GROUP):
+            to = place.member(j)
+            copy_out(j, to, g, part, lax.rem(to, 2)).wait_send()
     preduce.finish()
 
     proj = pfull[:, :basis] * cell_weight
@@ -520,13 +548,13 @@
             pltpu.SMEM(conductance.shape, f32),
             pltpu.SMEM(capacity_table.shape, f32),
             pltpu.SMEM(shift_values.shape, f32),
-            dma((3,)), dma((3,)), dma((GROUP - 1,)), dma((GROUP - 1,)),
-            dma((GROUP - 1,)), dma((GROUP - 1,)), dma((SWEEPS - 1, 2)), dma((SWEEPS - 1, 2)),
-            dma((8,)), dma((2, cells)), dma((cells,)),
+            dma((3,)), dma((3,)), dma((2, GROUP - 1)), dma((2, GROUP - 1)),
+            dma((2, GROUP - 1)), dma((2, GROUP - 1)), dma((SWEEPS - 1, 2)), dma((SWEEPS - 1, 2)),
+            dma((10,)), dma((2, cells)), dma((cells,)),
             dma((6, width)), dma((6, width)),
         ],
         compiler_params=pltpu.CompilerParams(
-            collective_id=0, has_side_effects=True, vmem_limit_bytes=48 * 1024 * 1024),
+            collective_id=0, has_side_effects=True, vmem_limit_bytes=64 * 1024 * 1024),
     )(labels, conductance, capacity_table, shift_values, prior_basis)
     return block.reshape(shifts, COLS, slab_x, quarter, depth), coef, factor
 

time: 90.5 us -> 83.1 us (0.918)
  Pallas kernels: 82.4 us -> 77.1 us
  local copies, waits for them, and re-layouts: 7.2 us -> 5.11 us
    pallas_call x1, Pallas kernels: 82.4 us -> 77.1 us  [local(): pl.pallas_call(functools.partial(kernel, slabs, 1.0 / count), out_shape=[...]
    unnamed x13 -> x3, local copies, waits for them, and re-layouts: 7.2 us -> 5.11 us
where the time goes in v4:
time: 83.1 us; the launch traced here: 82.8 us
  Pallas kernels  77.1 us (93%)
  local copies, waits for them, and re-layouts  5.11 us (6%)
    pallas_call x1, Pallas kernels, local(): pl.pallas_call(functools.partial(kernel, slabs, 1.0 / count), out_shape=[...  77.1 us
    unnamed x3, local copies, waits for them, and re-layouts  5.11 us

profile of v4, /device:TPU:0, one launch (start us, length us, event | category | flops | bytes accessed | tf_op | source)
XLA Modules:
  0.0 82.8 jit_solution(8321184508864073515)
XLA Ops:
  0.6 77.1 %shard_map.76 = (f32[64,2,8,256]{3,2,1,0:T(8,128)}, f32[64,256]{1,0:T(8,128)}, f32[64,64]{1,0:T(8,128)}) custom-call(s32[2,32,256]{2,1,0:T(8,128)} %labels_hbm.1, f32[8]{0:T(128)} %cond_hbm.1, f32[8]{0:T(128)} %capa_hbm.1, f32[8]{0:T(128)} %shift_hbm.1, f32[256,2,8,256]{3,2,1,0:T(8,128)} %q_hbm.1), custom_call_target="tpu_custom_call" | custom-call | tf_op jit(solution)/shard_map/pallas_call | solution.py:519
  77.7 2.3 %copy.11 = f32[8,8,2,8,256]{4,3,2,1,0:T(8,128)} copy(f32[8,8,2,8,256]{4,3,2,1,0:T(8,128)} %bitcast.1) | data formatting | bytes 2097152
  80.0 1.5 %copy.12 = f32[64,256]{1,0:T(8,128)} copy(f32[64,256]{1,0:T(8,128)} %get-tuple-element.13) | data formatting | bytes 131072
  81.5 1.4 %copy.13 = f32[64,64]{1,0:T(8,128)} copy(f32[64,64]{1,0:T(8,128)} %get-tuple-element.14) | data formatting | bytes 32768

commit v5 on v4

--- a/solution.py
+++ b/solution.py
@@ -382,12 +382,6 @@
         sweep(n, 2, keep, step)
         if n == SWEEPS - 2:
             send_out(1)
-        if n == 0:
-            greduce.start2()
-        if n == 1:
-            greduce.start3()
-        if n == 2:
-            greduce.finish()
 
         @pl.when(z > 0)
         def _():
@@ -403,6 +397,7 @@
             send_halo(n + 1)
 
     send_out(0)
+    greduce.start2()
 
     lab_pair(b).wait_send()
 
@@ -445,8 +440,10 @@
 
     preduce = Reducer(place, psrc, pfirst, psecond, pfull, [psem.at[i] for i in range(6)])
     preduce.start1()
+    greduce.start3()
     preduce.start2()
     preduce.start3()
+    greduce.finish()
     for part in (0, 1):
         for j in range(1, GROUP):
             to = place.member(j)

time: 83.1 us -> 80.5 us (0.969)
  Pallas kernels: 77.1 us -> 74.5 us
    pallas_call x1, Pallas kernels: 77.1 us -> 74.5 us  [local(): pl.pallas_call(functools.partial(kernel, slabs, 1.0 / count), out_shape=[...]
where the time goes in v5:
time: 80.5 us; the launch traced here: 80.2 us
  Pallas kernels  74.5 us (93%)
  local copies, waits for them, and re-layouts  5.11 us (6%)
    pallas_call x1, Pallas kernels, local(): pl.pallas_call(functools.partial(kernel, slabs, 1.0 / count), out_shape=[...  74.5 us
    unnamed x3, local copies, waits for them, and re-layouts  5.11 us

profile of v5, /device:TPU:0, one launch (start us, length us, event | category | flops | bytes accessed | tf_op | source)
XLA Modules:
  0.0 80.2 jit_solution(655930921948001048)
XLA Ops:
  0.6 74.5 %shard_map.76 = (f32[64,2,8,256]{3,2,1,0:T(8,128)}, f32[64,256]{1,0:T(8,128)}, f32[64,64]{1,0:T(8,128)}) custom-call(s32[2,32,256]{2,1,0:T(8,128)} %labels_hbm.1, f32[8]{0:T(128)} %cond_hbm.1, f32[8]{0:T(128)} %capa_hbm.1, f32[8]{0:T(128)} %shift_hbm.1, f32[256,2,8,256]{3,2,1,0:T(8,128)} %q_hbm.1), custom_call_target="tpu_custom_call" | custom-call | tf_op jit(solution)/shard_map/pallas_call | solution.py:516
  75.1 2.3 %copy.11 = f32[8,8,2,8,256]{4,3,2,1,0:T(8,128)} copy(f32[8,8,2,8,256]{4,3,2,1,0:T(8,128)} %bitcast.1) | data formatting | bytes 2097152
  77.4 1.5 %copy.12 = f32[64,256]{1,0:T(8,128)} copy(f32[64,256]{1,0:T(8,128)} %get-tuple-element.13) | data formatting | bytes 131072
  78.9 1.4 %copy.13 = f32[64,64]{1,0:T(8,128)} copy(f32[64,64]{1,0:T(8,128)} %get-tuple-element.14) | data formatting | bytes 32768
